TPU v7x, 768 devices: a whole 4x8x12 slice. The times are simulated.
768 devices in a mesh: row: 64 (over x, y, core), col: 12 (over z).
Axes of the slice: x: 4, y: 8, z: 12, core: 2. Of those that a mesh axis runs over, the one named last changes fastest.
Arguments:
- object_field: float32 [2, 2, 16384, 3072], P(None, None, 'row', 'col'), may hold values from -4 to 4
- probe: float32 [2, 2, 256, 256], replicated, may hold values from -3 to 3
- scan_positions: int32 [64, 12, 1, 2], P('row', 'col'), may hold values from 0 to 16128, as said below
- amplitudes: float32 [64, 12, 1, 256, 256], P('row', 'col'), may hold values from 0.2 to 1.8
Outputs:
- object_gradient: float32 [2, 2, 16384, 3072], P(None, None, 'row', 'col')
- probe_gradient: float32 [2, 2, 256, 256], replicated
Inputs may be any that keep to these rules, and one draw needn't show every extreme that they name: scan_positions[i, j, n] holds the row and the column of the upper left pixel of a 256 x 256 patch; the row lies in [i * 256, i * 256 + 256), the column in [j * 256, j * 256 + 256), and every patch lies inside the object; position 0 of device (0, 0) is at (0, 0) and position 0 of the last device is at (16128, 2816).
All inputs are finite; a program needn't handle non-finite values.
Results may differ from a plain program's by a relative error of at most 0.0003.
Values sent between devices are 32-bit elements; how exact they have to be, the bound alone decides.
A program may use at most 32 MiB of HBM per device.

v0:
```python
import math

import jax
import jax.numpy as jnp
from jax import lax
from jax.sharding import PartitionSpec as P

intensity_floor = 0.5
chirp_divisor = 2.0


def from_behind(array, axis, by):
    count = lax.axis_size(axis)
    pairs = [(i, i + by) for i in range(count) if 0 <= i + by < count]
    return lax.ppermute(array, axis, pairs)


def complex_blocks(matrix_real, matrix_imag):
    left_block = jnp.stack(
        [
            jnp.stack([matrix_real, -matrix_imag], axis=1),
            jnp.stack([matrix_imag, matrix_real], axis=1),
        ],
        axis=0,
    )
    real_t = matrix_real.T
    imag_t = matrix_imag.T
    right_block = jnp.stack(
        [jnp.stack([real_t, imag_t], axis=1), jnp.stack([-imag_t, real_t], axis=1)], axis=0
    )
    return (left_block, right_block)


def tables(order_dft):
    indices = jnp.arange(order_dft, dtype=jnp.int32)
    products = indices[:, None] * indices[None, :] % order_dft
    angles = 2.0 * math.pi / order_dft * products.astype(jnp.float32)
    norm_factor = 1.0 / math.sqrt(order_dft)
    dft_real = jnp.cos(angles) * norm_factor
    dft_imag = -jnp.sin(angles) * norm_factor
    centered = jnp.where(indices < order_dft // 2, indices, indices - order_dft).astype(jnp.float32)
    chirp_phase = -math.pi * centered * centered / (chirp_divisor * order_dft)
    phase_real = jnp.cos(chirp_phase)
    phase_imag = jnp.sin(chirp_phase)
    shifted_real = phase_real[:, None] * dft_real - phase_imag[:, None] * dft_imag
    shifted_imag = phase_real[:, None] * dft_imag + phase_imag[:, None] * dft_real
    highest = lax.Precision.HIGHEST
    kernel_real = jnp.dot(dft_real, shifted_real, precision=highest) + jnp.dot(
        dft_imag, shifted_imag, precision=highest
    )
    kernel_imag = jnp.dot(dft_real, shifted_imag, precision=highest) - jnp.dot(
        dft_imag, shifted_real, precision=highest
    )
    dft_left, dft_right = complex_blocks(dft_real, dft_imag)
    kernel_left, kernel_right = complex_blocks(kernel_real, kernel_imag)
    return (dft_left, dft_right, kernel_left, kernel_right)


def apply_both(left_block, right_block, field):
    highest = lax.Precision.HIGHEST
    field = jnp.einsum("satb,mtbc->msac", left_block, field, precision=highest)
    return jnp.einsum("mtab,tbsc->msac", field, right_block, precision=highest)


def complex_times(field, factor):
    out_real = field[:, 0] * factor[0] - field[:, 1] * factor[1]
    out_imag = field[:, 0] * factor[1] + field[:, 1] * factor[0]
    return jnp.stack([out_real, out_imag], axis=1)


def position_loss(probe, object_patch, amplitude_block, tables_dft):
    dft_left, dft_right, kernel_left, kernel_right = tables_dft
    wave = complex_times(probe, object_patch[0])
    wave = apply_both(kernel_left, kernel_right, wave)
    wave = complex_times(wave, object_patch[1])
    far = apply_both(dft_left, dft_right, wave)
    intensity = jnp.sum(far * far, axis=(0, 1))
    return jnp.sum((jnp.sqrt(intensity + intensity_floor) - amplitude_block) ** 2)


def position_grads(probe, object_patch, amplitude_block, tables_dft):
    misfit, pullback = jax.vjp(
        lambda probe_in, patch_in: position_loss(probe_in, patch_in, amplitude_block, tables_dft),
        probe,
        object_patch,
    )
    return pullback(jnp.ones_like(misfit))


def on_device(object_field, probe, scan_positions, amplitudes):
    layers, halves, tile_rows, tile_cols = object_field.shape
    probe_width = probe.shape[-1]
    tables_dft = tables(probe_width)
    right_rim = from_behind(object_field, "col", -1)
    widened = jnp.concatenate([object_field, right_rim], axis=3)
    below_rim = from_behind(widened, "row", -1)
    extended = jnp.concatenate([widened, below_rim], axis=2)
    row_base = lax.axis_index("row") * tile_rows
    col_base = lax.axis_index("col") * tile_cols
    anchor = jnp.zeros((), jnp.int32)
    object_grads = jnp.zeros(extended.shape, jnp.float32)
    position_count = scan_positions.shape[2]
    corner = scan_positions[0, 0, 0]
    row_start = corner[0] - row_base
    col_start = corner[1] - col_base
    corner_start = (anchor, anchor, row_start, col_start)
    object_patch = lax.dynamic_slice(
        extended, corner_start, (layers, halves, probe_width, probe_width)
    )
    probe_part, patch_part = position_grads(probe, object_patch, amplitudes[0, 0, 0], tables_dft)
    object_grads = lax.dynamic_update_slice(object_grads, patch_part, corner_start)
    from_above = from_behind(object_grads[:, :, tile_rows:, :], "row", 1)
    upper_rows = object_grads[:, :, :tile_rows, :].at[:, :, :probe_width, :].add(from_above)
    from_left = from_behind(upper_rows[:, :, :, tile_cols:], "col", 1)
    object_gradient = upper_rows[:, :, :, :tile_cols].at[:, :, :, :probe_width].add(from_left)
    position_total = position_count * lax.axis_size("row") * lax.axis_size("col")
    summed_probe = lax.psum(probe_part, ("row", "col"))
    probe_gradient = summed_probe / math.sqrt(position_total)
    return (object_gradient, probe_gradient)


def solution(mesh):
    in_specs = (
        P(None, None, "row", "col"),
        P(),
        P("row", "col", None, None),
        P("row", "col", None, None, None),
    )
    out_specs = (P(None, None, "row", "col"), P())
    return jax.shard_map(
        on_device, mesh=mesh, in_specs=in_specs, out_specs=out_specs, check_vma=False
    )
```

profile of v0, /device:TPU:1, one launch (start us, length us, event | category | flops | bytes accessed | tf_op | source)
XLA Modules:
  0.0 630.3 jit_solution(3233700660328839276)
XLA Ops:
  14.0 12.5 %collective-permute-done = f32[2,2,256,256]{3,2,1,0:T(8,128)} collective-permute-done((f32[2,2,256,256]{3,2,1,0:T(8,128)}, f32[2,2,256,256]{3,2,1,0:T(8,128)}, u32[]{:S(2)}, u32[]{:S(2)}) %collective-permute-start) | collective-permute-done | bytes 1048608 | tf_op jit(solution)/shard_map/ppermute | solution.py:15
  27.8 11.9 %collective-permute-start.1 = (f32[2,2,256,512]{3,2,1,0:T(8,128)S(1)}, f32[2,2,256,512]{3,2,1,0:T(8,128)S(1)}, u32[]{:S(2)}, u32[]{:S(2)}) collective-permute-start(f32[2,2,256,512]{3,2,1,0:T(8,128)S(1)} %constant_dynamic-update-slice_fusion), channel_id=1, source_target_pairs={{12,0},{24,12},{36,24},{48,36},{60,48},{72,60},{84,72},{96,84},{10... | collective-permute-start | bytes 6291464 | tf_op jit(solution)/shard_map/ppermute | solution.py:15
  43.2 1.5 fusion.48
  46.3 1.5 convolution_add_fusion
  49.3 15.3 %collective-permute-done.1 = f32[2,2,256,512]{3,2,1,0:T(8,128)S(1)} collective-permute-done((f32[2,2,256,512]{3,2,1,0:T(8,128)S(1)}, f32[2,2,256,512]{3,2,1,0:T(8,128)S(1)}, u32[]{:S(2)}, u32[]{:S(2)}) %collective-permute-start.1) | collective-permute-done | bytes 2097184 | tf_op jit(solution)/shard_map/ppermute | solution.py:15
  67.4 1.8 copy.31
  69.2 1.8 copy.37
  71.0 1.8 copy.38
  73.8 1.9 convolution_bitcast_fusion.7
  75.7 2.1 convolution_bitcast_fusion.6
  79.0 1.9 convolution_bitcast_fusion.5
  80.9 1.9 multiply_reduce_fusion
  82.9 1.9 convolution_bitcast_fusion.3
  84.9 1.9 convolution_bitcast_fusion.2
  87.1 2.1 convolution_bitcast_fusion.1
  89.3 1.8 convolution_bitcast_fusion
  91.9 2.5 broadcast_in_dim.10
  94.4 11.8 %dynamic_update_slice.3 = f32[2,2,512,512]{3,2,1,0:T(8,128)} dynamic-update-slice(f32[2,2,512,512]{3,2,1,0:T(8,128)} %broadcast_in_dim.10, f32[2,2,256,256]{3,2,1,0:T(8,128)S(1)} %copy.45, s32[]{:T(128)} %constant.101.clone.1, s32[]{:T(128)} %constant.101.clone.1, s32[]{:T(128)S(6)} %select_n.84, s32[]{:T(128)S(6)} %select_n.85) | dynamic-update-slice | bytes 2097156 | tf_op jit(solution)/shard_map/dynamic_update_slice | solution.py:111
  106.2 1.9 slice.131
  108.1 1.9 collective-permute-start.2
  110.0 23.0 %collective-permute-done.2 = f32[2,2,256,512]{3,2,1,0:T(8,128)S(1)} collective-permute-done((f32[2,2,256,512]{3,2,1,0:T(8,128)S(1)}, f32[2,2,256,512]{3,2,1,0:T(8,128)S(1)}, u32[]{:S(2)}, u32[]{:S(2)}) %collective-permute-start.2) | collective-permute-done | bytes 2097184 | tf_op jit(solution)/shard_map/ppermute | solution.py:15
  134.5 4.9 collective-permute-start.3
  140.7 477.7 %all-reduce.20.cloned.1.call-done = f32[2,2,256,256]{2,3,1,0:T(8,128)} async-done(((f32[2,2,256,256]{2,3,1,0:T(8,128)}), f32[2,2,256,256]{2,3,1,0:T(8,128)}) %all-reduce.20.cloned.1.call-update) | async-done | bytes 1048592 | tf_op jit(solution)/shard_map/psum | solution.py:117
  621.0 2.4 slice_add_fusion.1
  (62 shorter events, 25.1 us)
Async XLA Ops:
  7.2 611.2 %all-reduce.20.cloned.1.call-start = ((), (), s32[]{:S(2)}) async-start(), calls=%async_computation | async-start | bytes 2097152 | tf_op jit(solution)/shard_map/psum | solution.py:117
  7.2 19.3 %collective-permute-start = (f32[2,2,256,256]{3,2,1,0:T(8,128)}, f32[2,2,256,256]{3,2,1,0:T(8,128)}, u32[]{:S(2)}, u32[]{:S(2)}) collective-permute-start(f32[2,2,256,256]{3,2,1,0:T(8,128)} %param.12), channel_id=1, source_target_pairs={{1,0},{2,1},{3,2},{4,3},{5,4},{6,5},{7,6},{8,7},{9,8},{10,9},{11,1... | collective-permute-start | bytes 3145736 | tf_op jit(solution)/shard_map/ppermute | solution.py:15
  11.1 1.8 copy-start.10
  11.2 2.7 copy-start.9
  27.8 36.8 %collective-permute-start.1 = (f32[2,2,256,512]{3,2,1,0:T(8,128)S(1)}, f32[2,2,256,512]{3,2,1,0:T(8,128)S(1)}, u32[]{:S(2)}, u32[]{:S(2)}) collective-permute-start(f32[2,2,256,512]{3,2,1,0:T(8,128)S(1)} %constant_dynamic-update-slice_fusion), channel_id=1, source_target_pairs={{12,0},{24,12},{36,24},{48,36},{60,48},{72,60},{84,72},{96,84},{10... | collective-permute-start | bytes 6291464 | tf_op jit(solution)/shard_map/ppermute | solution.py:15
  75.7 2.1 copy-start.6
  75.7 2.1 copy-start.7
  77.8 1.0 copy-start.1
  77.8 1.2 copy-start.2
  77.9 2.9 copy-start.3
  77.9 2.9 copy-start.4
  80.9 1.9 copy-start.8
  106.2 26.8 %copy-start = (f32[2,2,512,512]{3,2,1,0:T(8,128)S(1)}, f32[2,2,512,512]{3,2,1,0:T(8,128)}, u32[]{:S(2)}) copy-start(f32[2,2,512,512]{3,2,1,0:T(8,128)} %dynamic_update_slice.3) | copy-start | bytes 12582916
  108.1 24.9 %collective-permute-start.2 = (f32[2,2,256,512]{3,2,1,0:T(8,128)S(1)}, f32[2,2,256,512]{3,2,1,0:T(8,128)S(1)}, u32[]{:S(2)}, u32[]{:S(2)}) collective-permute-start(f32[2,2,256,512]{3,2,1,0:T(8,128)S(1)} %slice.131), channel_id=1, source_target_pairs={{0,12},{12,24},{24,36},{36,48},{48,60},{60,72},{72,84},{84,96},{96... | collective-permute-start | bytes 6291464 | tf_op jit(solution)/shard_map/ppermute | solution.py:15
  133.5 5.9 copy-start.5
  134.5 486.5 %collective-permute-start.3 = (f32[2,2,256,256]{3,2,1,0:T(8,128)}, f32[2,2,256,256]{3,2,1,0:T(8,128)}, u32[]{:S(2)}, u32[]{:S(2)}) collective-permute-start(f32[2,2,256,256]{3,2,1,0:T(8,128)} %slice.133), channel_id=1, source_target_pairs={{0,1},{1,2},{2,3},{3,4},{4,5},{5,6},{6,7},{7,8},{8,9},{9,10},{10,1... | collective-permute-start | bytes 3145736 | tf_op jit(solution)/shard_map/ppermute | solution.py:15
Sparse Core Ops, SparseCore 0:
  140.8 477.5 all-reduce.19
where the time goes:
time: 632 us; the launch traced here: 630 us
  waiting for transfers between devices  528 us (84%)
  local copies, waits for them, and re-layouts  32.8 us (5%)
  matrix products  21.4 us (3%)
  starting transfers between devices  20 us (3%)
  between operations  15.8 us (2%)
  other arithmetic  11.8 us (2%)
    psum x1, waiting for transfers between devices, on_device(): summed_probe = lax.psum(probe_part, ('row', 'col'))  478 us
    ppermute x4, waiting for transfers between devices, from_behind(): return lax.ppermute(array, axis, pairs)  50.7 us
    ppermute x4, starting transfers between devices, from_behind(): return lax.ppermute(array, axis, pairs)  20 us
  transfers between devices with their start and end apart: 5, of which 4 were waited for; matrix products, arithmetic and copies ran while one was open for 3% of the time, Pallas kernels for 0%

commit v1 on v0

--- a/solution.py
+++ b/solution.py
@@ -3,10 +3,165 @@
 import jax
 import jax.numpy as jnp
 from jax import lax
+from jax.experimental import pallas as pl
+from jax.experimental.pallas import tpu as pltpu
 from jax.sharding import PartitionSpec as P
 
 intensity_floor = 0.5
 chirp_divisor = 2.0
+MESH_ID = pl.DeviceIdType.MESH
+
+
+def place():
+    row = lax.axis_index("row")
+    return row // 16, (row // 2) % 8, lax.axis_index("col"), row % 2
+
+
+def device(x, y, z, core):
+    return ((x * 8 + y) * 2 + core, z)
+
+
+def start_copy(source, target, sent, landed, to):
+    copy = pltpu.make_async_remote_copy(
+        src_ref=source, dst_ref=target, send_sem=sent, recv_sem=landed, device_id=to, device_id_type=MESH_ID
+    )
+    copy.start()
+
+
+def wait_bytes(ref, semaphore):
+    pltpu.make_async_copy(ref, ref, semaphore).wait()
+
+
+class ProbeSum:
+    def __init__(self, parts, total, from_core, near, from_x, mid, from_y, from_z, sent, landed, scale):
+        self.parts, self.total, self.from_core, self.near = parts, total, from_core, near
+        self.from_x, self.mid, self.from_y, self.from_z = from_x, mid, from_y, from_z
+        self.sent, self.landed, self.scale = sent, landed, scale
+        self.x, self.y, self.z, self.core = place()
+
+    def x_peers(self):
+        return [lax.rem(self.x + d, 4) for d in range(1, 4)]
+
+    def y_peers(self):
+        return [lax.rem(self.y + d, 8) for d in range(1, 8)]
+
+    def z_peers(self):
+        return [lax.rem(self.z + d, 12) for d in range(1, 12)]
+
+    def columns(self, chunk):
+        return chunk // 2, pl.ds(128 * (chunk % 2), 128)
+
+    def stage(self, chunk, step):
+        x, y, z, core = self.x, self.y, self.z, self.core
+        mode, lanes = self.columns(chunk)
+        other = device(x, y, z, 1 - core)
+        sent, landed = self.sent.at[chunk, step], self.landed.at[chunk, step]
+        arrived = self.landed.at[chunk, step - 1]
+        mine = pl.ds(pl.multiple_of(64 * x + 8 * y, 8), 8)
+        block = pl.ds(pl.multiple_of(64 * x, 64), 64)
+        if step == 0:
+            start_copy(self.parts.at[mode, 1 - core, :, lanes], self.from_core.at[chunk], sent, landed, other)
+        elif step == 1:
+            wait_bytes(self.from_core.at[chunk], arrived)
+            self.near[chunk] = self.parts[mode, core, :, lanes] + self.from_core[chunk]
+            for d, px in enumerate(self.x_peers()):
+                rows = pl.ds(pl.multiple_of(64 * px, 64), 64)
+                start_copy(self.near.at[chunk, rows], self.from_x.at[chunk, d], sent, landed, device(px, y, z, core))
+        elif step == 2:
+            wait_bytes(self.from_x.at[chunk], arrived)
+            self.mid[chunk] = (self.near[chunk, block, :] + self.from_x[chunk, 0]) + (
+                self.from_x[chunk, 1] + self.from_x[chunk, 2]
+            )
+            for d, py in enumerate(self.y_peers()):
+                rows = pl.ds(pl.multiple_of(8 * py, 8), 8)
+                start_copy(self.mid.at[chunk, rows], self.from_y.at[chunk, d], sent, landed, device(x, py, z, core))
+        elif step == 3:
+            wait_bytes(self.from_y.at[chunk], arrived)
+            piece = self.mid[chunk, pl.ds(pl.multiple_of(8 * y, 8), 8), :]
+            for d in range(7):
+                piece = piece + self.from_y[chunk, d]
+            self.from_z[chunk, z] = piece
+            for pz in self.z_peers():
+                start_copy(self.from_z.at[chunk, z], self.from_z.at[chunk, z], sent, landed, device(x, y, pz, core))
+        elif step == 4:
+            wait_bytes(self.from_z.at[chunk, pl.ds(0, 11)], arrived)
+            piece = self.from_z[chunk, 0]
+            for d in range(1, 12):
+                piece = piece + self.from_z[chunk, d]
+            self.total[mode, core, mine, lanes] = piece * self.scale
+            spot = self.total.at[mode, core, mine, lanes]
+            for py in self.y_peers():
+                start_copy(spot, spot, sent, landed, device(x, py, z, core))
+        elif step == 5:
+            wait_bytes(self.total.at[mode, core, pl.ds(0, 56), lanes], arrived)
+            spot = self.total.at[mode, core, block, lanes]
+            for px in self.x_peers():
+                start_copy(spot, spot, sent, landed, device(px, y, z, core))
+        elif step == 6:
+            wait_bytes(self.total.at[mode, core, pl.ds(0, 192), lanes], arrived)
+            spot = self.total.at[mode, core, :, lanes]
+            start_copy(spot, spot, sent, landed, other)
+        elif step == 7:
+            wait_bytes(self.total.at[mode, core, :, lanes], arrived)
+
+    def drain(self, chunk):
+        mode, lanes = self.columns(chunk)
+        sizes = [
+            self.from_core.at[chunk],
+            self.from_x.at[chunk],
+            self.from_y.at[chunk],
+            self.from_z.at[chunk, pl.ds(0, 11)],
+            self.total.at[mode, self.core, pl.ds(0, 56), lanes],
+            self.total.at[mode, self.core, pl.ds(0, 192), lanes],
+            self.total.at[mode, self.core, :, lanes],
+        ]
+        for step, ref in enumerate(sizes):
+            wait_bytes(ref, self.sent.at[chunk, step])
+
+    def greet(self, barrier):
+        x, y, z, core = self.x, self.y, self.z, self.core
+        peers = [device(x, y, z, 1 - core)]
+        peers += [device(px, y, z, core) for px in self.x_peers()]
+        peers += [device(x, py, z, core) for py in self.y_peers()]
+        peers += [device(x, y, pz, core) for pz in self.z_peers()]
+        for peer in peers:
+            pl.semaphore_signal(barrier, inc=1, device_id=peer, device_id_type=MESH_ID)
+        return len(peers)
+
+
+PROBE_SUM_SCRATCH = [
+    pltpu.VMEM((4, 256, 128), jnp.float32),
+    pltpu.VMEM((4, 256, 128), jnp.float32),
+    pltpu.VMEM((4, 3, 64, 128), jnp.float32),
+    pltpu.VMEM((4, 64, 128), jnp.float32),
+    pltpu.VMEM((4, 7, 8, 128), jnp.float32),
+    pltpu.VMEM((4, 12, 8, 128), jnp.float32),
+    pltpu.SemaphoreType.DMA((4, 7)),
+    pltpu.SemaphoreType.DMA((4, 7)),
+]
+
+
+def probe_sum_kernel(parts, total, *scratch):
+    total_sum = ProbeSum(parts, total, *scratch, 1.0 / math.sqrt(768))
+    barrier = pltpu.get_barrier_semaphore()
+    count = total_sum.greet(barrier)
+    pl.semaphore_wait(barrier, count)
+    for step in range(8):
+        for chunk in range(4):
+            total_sum.stage(chunk, step)
+    for chunk in range(4):
+        total_sum.drain(chunk)
+
+
+def probe_sum(parts):
+    return pl.pallas_call(
+        probe_sum_kernel,
+        out_shape=jax.ShapeDtypeStruct((2, 2, 256, 256), jnp.float32),
+        in_specs=[pl.BlockSpec(memory_space=pltpu.VMEM)],
+        out_specs=pl.BlockSpec(memory_space=pltpu.VMEM),
+        scratch_shapes=PROBE_SUM_SCRATCH,
+        compiler_params=pltpu.CompilerParams(collective_id=0, has_side_effects=True, vmem_limit_bytes=32 << 20),
+    )(parts)
 
 
 def from_behind(array, axis, by):
@@ -99,7 +254,6 @@
     col_base = lax.axis_index("col") * tile_cols
     anchor = jnp.zeros((), jnp.int32)
     object_grads = jnp.zeros(extended.shape, jnp.float32)
-    position_count = scan_positions.shape[2]
     corner = scan_positions[0, 0, 0]
     row_start = corner[0] - row_base
     col_start = corner[1] - col_base
@@ -113,9 +267,7 @@
     upper_rows = object_grads[:, :, :tile_rows, :].at[:, :, :probe_width, :].add(from_above)
     from_left = from_behind(upper_rows[:, :, :, tile_cols:], "col", 1)
     object_gradient = upper_rows[:, :, :, :tile_cols].at[:, :, :, :probe_width].add(from_left)
-    position_total = position_count * lax.axis_size("row") * lax.axis_size("col")
-    summed_probe = lax.psum(probe_part, ("row", "col"))
-    probe_gradient = summed_probe / math.sqrt(position_total)
+    probe_gradient = probe_sum(probe_part)
     return (object_gradient, probe_gradient)
 
 

time: 632 us -> 194 us (0.31)
  waiting for transfers between devices: 528 us -> 48.8 us
  Pallas kernels: 0 us -> 58.4 us
  between operations: 15.8 us -> 2.47 us
    psum x1 -> x0, waiting for transfers between devices: 478 us -> none  [on_device(): summed_probe = lax.psum(probe_part, ('row', 'col'))]
    pallas_call x0 -> x1, Pallas kernels: none -> 58.4 us  [probe_sum(): pl.pallas_call(probe_sum_kernel, out_shape=jax.ShapeDtypeStruct((2, 2, 25...]
  transfers between devices with their start and end apart: 5 -> 4, of which waited for: 4 -> 3; matrix products, arithmetic and copies ran while one was open for 3% -> 8% of each run, Pallas kernels for 0% -> 30%
where the time goes in v1:
time: 194 us; the launch traced here: 193 us
  Pallas kernels  58.4 us (30%)
  waiting for transfers between devices  48.8 us (25%)
  local copies, waits for them, and re-layouts  28.1 us (14%)
  matrix products  24.7 us (13%)
  starting transfers between devices  19.4 us (10%)
  other arithmetic  10.8 us (6%)
  between operations  2.47 us (1%)
    pallas_call x1, Pallas kernels, probe_sum(): pl.pallas_call(probe_sum_kernel, out_shape=jax.ShapeDtypeStruct((2, 2, 25...  58.4 us
    ppermute x4, waiting for transfers between devices, from_behind(): return lax.ppermute(array, axis, pairs)  48.8 us
    ppermute x4, starting transfers between devices, from_behind(): return lax.ppermute(array, axis, pairs)  19.4 us
    dynamic_update_slice x1, local copies, waits for them, and re-layouts, on_device(): lax.dynamic_update_slice(object_grads, patch_part, corner_start)  11.8 us
    dot_general x4, matrix products, apply_both(): return jnp.einsum('mtab,tbsc->msac', field, right_block, precision=highest)  9.65 us
    dot_general x4, matrix products, apply_both(): field = jnp.einsum('satb,mtbc->msac', left_block, field, precision=highest)  9.15 us
    unnamed x33, local copies, waits for them, and re-layouts  5.55 us
    mul x3, local copies, waits for them, and re-layouts, complex_times(): out_real = field[:, 0] * factor[0] - field[:, 1] * factor[1]  3.9 us
  transfers between devices with their start and end apart: 4, of which 3 were waited for; matrix products, arithmetic and copies ran while one was open for 8% of the time, Pallas kernels for 30%

profile of v1, /device:TPU:1, one launch (start us, length us, event | category | flops | bytes accessed | tf_op | source)
XLA Modules:
  0.0 192.7 jit_solution(2999268237931488708)
XLA Ops:
  4.6 1.8 copy.60
  10.7 9.2 %collective-permute-done = f32[2,2,256,256]{3,2,1,0:T(8,128)S(1)} collective-permute-done((f32[2,2,256,256]{3,2,1,0:T(8,128)}, f32[2,2,256,256]{3,2,1,0:T(8,128)S(1)}, u32[]{:S(2)}, u32[]{:S(2)}) %collective-permute-start) | collective-permute-done | bytes 1048608 | tf_op jit(solution)/shard_map/ppermute | solution.py:170
  19.9 12.1 %collective-permute-start.1 = (f32[2,2,256,512]{3,2,1,0:T(8,128)S(1)}, f32[2,2,256,512]{3,2,1,0:T(8,128)S(1)}, u32[]{:S(2)}, u32[]{:S(2)}) collective-permute-start(f32[2,2,256,512]{3,2,1,0:T(8,128)S(1)} %constant_dynamic-update-slice_fusion), channel_id=1, source_target_pairs={{12,0},{24,12},{36,24},{48,36},{60,48},{72,60},{84,72},{96,84},{10... | collective-permute-start | bytes 6291464 | tf_op jit(solution)/shard_map/ppermute | solution.py:170
  32.0 1.5 fusion.42
  33.5 1.5 fusion.44
  35.0 1.5 convolution_subtract_fusion
  38.4 1.6 maximum_bitcast_fusion.3
  40.0 16.7 %collective-permute-done.1 = f32[2,2,256,512]{3,2,1,0:T(8,128)S(1)} collective-permute-done((f32[2,2,256,512]{3,2,1,0:T(8,128)S(1)}, f32[2,2,256,512]{3,2,1,0:T(8,128)S(1)}, u32[]{:S(2)}, u32[]{:S(2)}) %collective-permute-start.1) | collective-permute-done | bytes 2097184 | tf_op jit(solution)/shard_map/ppermute | solution.py:170
  59.5 1.8 copy.55
  62.7 3.5 %convolution_bitcast_fusion.7 = f32[2,2,256,256,1]{2,3,1,0,4:T(8,128)S(1)} fusion(f32[1,256,2,256]{3,1,2,0:T(8,128)S(1)} %get-tuple-element.79, f32[1,256,2,256]{3,1,2,0:T(8,128)S(1)} %get-tuple-element.78, f32[2,1,256,256]{3,2,0,1:T(8,128)S(1)} %get-tuple-element.53, f32[2,1,256,256]{3,2,0,1:T(8,128)S(1)} %get-tuple-element.52), kind=kOutput, calls=%fused_computation.10 | convolution fusion | flops 1611137024 | bytes 3145728 | tf_op jit(solution)/shard_map/jvp(satb,mtbc->msac)/dot_general | solution.py:216
  66.2 2.1 %convolution_bitcast_fusion.6 = f32[2,2,256,256]{2,3,0,1:T(8,128)S(1)} fusion(f32[2,2,256,256,1]{2,3,1,0,4:T(8,128)S(1)} %convolution_bitcast_fusion.7, f32[1,256,2,256]{1,3,2,0:T(8,128)S(1)} %get-tuple-element.77, f32[1,256,2,256]{1,3,2,0:T(8,128)S(1)} %get-tuple-element.76), kind=kOutput, calls=%fused_computation.9 | convolution fusion | flops 1610874880 | bytes 3145728 | tf_op jit(solution)/shard_map/jvp(mtab,tbsc->msac)/dot_general | solution.py:217
  69.5 1.9 convolution_bitcast_fusion.5
  71.4 1.9 multiply_reduce_fusion
  73.4 3.5 %convolution_bitcast_fusion.3 = f32[2,256,2,256,1]{1,3,2,0,4:T(8,128)S(1)} fusion(f32[1,256,2,256]{3,1,2,0:T(8,128)S(1)} %get-tuple-element.75, f32[1,256,2,256]{3,1,2,0:T(8,128)S(1)} %get-tuple-element.70, f32[2,256,2,256]{3,1,2,0:T(8,128)S(1)} %get-tuple-element.83, f32[256,256]{1,0:T(8,128)S(1)} %fusion.32), kind=kOutput, calls=%fused_computation.6 | convolution fusion | flops 1611399168 | bytes 3407872 | tf_op jit(solution)/shard_map/transpose(jvp(mtab,tbsc->msac))/dot_general | solution.py:217
  77.0 1.9 convolution_bitcast_fusion.2
  80.1 2.2 %convolution_bitcast_fusion.1 = f32[2,256,2,256,1]{1,3,2,0,4:T(8,128)S(1)} fusion(f32[1,256,2,256]{1,3,2,0:T(8,128)S(1)} %get-tuple-element.77, f32[1,256,2,256]{1,3,2,0:T(8,128)S(1)} %get-tuple-element.76, f32[2,1,256,256]{2,3,0,1:T(8,128)S(1)} %get-tuple-element.59, f32[2,1,256,256]{2,3,0,1:T(8,128)S(1)} %get-tuple-element.64, ...), kind=kOutput, calls=%fused_computation.4 | convolution fusion | flops 1611661312 | bytes 4194304 | tf_op jit(solution)/shard_map/transpose(jvp(mtab,tbsc->msac))/dot_general | solution.py:217
  82.3 1.9 convolution_bitcast_fusion
  85.9 2.5 %broadcast_in_dim.10 = f32[2,2,512,512]{3,2,1,0:T(8,128)} broadcast(f32[]{:T(128)} %constant.98.clone.1), dimensions={} | broadcast | bytes 4194308 | tf_op jit(solution)/shard_map/broadcast_in_dim | solution.py:256
  88.4 11.8 %dynamic_update_slice.3 = f32[2,2,512,512]{3,2,1,0:T(8,128)} dynamic-update-slice(f32[2,2,512,512]{3,2,1,0:T(8,128)} %broadcast_in_dim.10, f32[2,2,256,256]{3,2,1,0:T(8,128)S(1)} %copy.75, s32[]{:T(128)} %constant.99.clone.1, s32[]{:T(128)} %constant.99.clone.1, s32[]{:T(128)S(6)} %select_n.84, s32[]{:T(128)S(6)} %select_n.85) | dynamic-update-slice | bytes 2097156 | tf_op jit(solution)/shard_map/dynamic_update_slice | solution.py:265
  100.2 2.0 %slice.131 = f32[2,2,256,512]{3,2,1,0:T(8,128)S(1)} slice(f32[2,2,512,512]{3,2,1,0:T(8,128)} %dynamic_update_slice.3), slice={[0:2], [0:2], [256:512], [0:512]} | slice | bytes 4194304 | tf_op jit(solution)/shard_map/slice | solution.py:266
  102.2 1.9 collective-permute-start.2
  104.1 23.0 %collective-permute-done.2 = f32[2,2,256,512]{3,2,1,0:T(8,128)S(1)} collective-permute-done((f32[2,2,256,512]{3,2,1,0:T(8,128)S(1)}, f32[2,2,256,512]{3,2,1,0:T(8,128)S(1)}, u32[]{:S(2)}, u32[]{:S(2)}) %collective-permute-start.2) | collective-permute-done | bytes 2097184 | tf_op jit(solution)/shard_map/ppermute | solution.py:170
  127.7 4.1 %collective-permute-start.3 = (f32[2,2,256,256]{3,2,1,0:T(8,128)S(1)}, f32[2,2,256,256]{3,2,1,0:T(8,128)S(1)}, u32[]{:S(2)}, u32[]{:S(2)}) collective-permute-start(f32[2,2,256,256]{3,2,1,0:T(8,128)S(1)} %slice.133), channel_id=1, source_target_pairs={{0,1},{1,2},{2,3},{3,4},{4,5},{5,6},{6,7},{7,8},{8,9},{9,10},{10,1... | collective-permute-start | bytes 3145736 | tf_op jit(solution)/shard_map/ppermute | solution.py:170
  132.1 58.4 %shard_map.69 = f32[2,2,256,256]{3,2,1,0:T(8,128)S(1)} custom-call(f32[2,2,256,256]{3,2,1,0:T(8,128)S(1)} %pad_add_fusion.parts), custom_call_target="tpu_custom_call" | custom-call | tf_op jit(solution)/shard_map/pallas_call | solution.py:157
  (68 shorter events, 20.2 us)
Async XLA Ops:
  0.6 19.2 %collective-permute-start = (f32[2,2,256,256]{3,2,1,0:T(8,128)}, f32[2,2,256,256]{3,2,1,0:T(8,128)S(1)}, u32[]{:S(2)}, u32[]{:S(2)}) collective-permute-start(f32[2,2,256,256]{3,2,1,0:T(8,128)} %param.12), channel_id=1, source_target_pairs={{1,0},{2,1},{3,2},{4,3},{5,4},{6,5},{7,6},{8,7},{9,8},{10,9},{11,1... | collective-permute-start | bytes 3145736 | tf_op jit(solution)/shard_map/ppermute | solution.py:170
  19.9 36.8 %collective-permute-start.1 = (f32[2,2,256,512]{3,2,1,0:T(8,128)S(1)}, f32[2,2,256,512]{3,2,1,0:T(8,128)S(1)}, u32[]{:S(2)}, u32[]{:S(2)}) collective-permute-start(f32[2,2,256,512]{3,2,1,0:T(8,128)S(1)} %constant_dynamic-update-slice_fusion), channel_id=1, source_target_pairs={{12,0},{24,12},{36,24},{48,36},{60,48},{72,60},{84,72},{96,84},{10... | collective-permute-start | bytes 6291464 | tf_op jit(solution)/shard_map/ppermute | solution.py:170
  38.4 1.7 copy-start.1
  38.4 1.7 copy-start.3
  66.2 2.1 %copy-start.8 = (f32[256,256]{0,1:T(8,128)S(1)}, f32[256,256]{0,1:T(8,128)}, u32[]{:S(2)}) copy-start(f32[256,256]{0,1:T(8,128)} %copy.55) | copy-start | bytes 786436
  68.3 1.0 copy-start.2
  68.3 1.2 copy-start.4
  68.4 2.9 %copy-start.7 = (f32[2,256,2,256,1]{3,1,2,0,4:T(8,128)S(1)}, f32[2,256,2,256,1]{3,1,2,0,4:T(8,128)}, u32[]{:S(2)}) copy-start(f32[2,256,2,256,1]{3,1,2,0,4:T(8,128)} %get-tuple-element.86) | copy-start | bytes 3145732
  71.4 1.9 copy-start.11
  73.3 3.7 %copy-start.6 = (f32[2,256,2,256,1]{3,1,2,0,4:T(8,128)S(1)}, f32[2,256,2,256,1]{3,1,2,0,4:T(8,128)}, u32[]{:S(2)}) copy-start(f32[2,256,2,256,1]{3,1,2,0,4:T(8,128)} %get-tuple-element.87) | copy-start | bytes 3145732
  82.3 1.9 copy-start.5
  84.2 1.0 copy-start.12
  84.2 1.0 copy-start.13
  84.2 1.1 copy-start.14
  100.2 26.9 %copy-start = (f32[2,2,512,512]{3,2,1,0:T(8,128)S(1)}, f32[2,2,512,512]{3,2,1,0:T(8,128)}, u32[]{:S(2)}) copy-start(f32[2,2,512,512]{3,2,1,0:T(8,128)} %dynamic_update_slice.3) | copy-start | bytes 12582916
  102.2 24.9 %collective-permute-start.2 = (f32[2,2,256,512]{3,2,1,0:T(8,128)S(1)}, f32[2,2,256,512]{3,2,1,0:T(8,128)S(1)}, u32[]{:S(2)}, u32[]{:S(2)}) collective-permute-start(f32[2,2,256,512]{3,2,1,0:T(8,128)S(1)} %slice.131), channel_id=1, source_target_pairs={{0,12},{12,24},{24,36},{36,48},{48,60},{60,72},{72,84},{84,96},{96... | collective-permute-start | bytes 6291464 | tf_op jit(solution)/shard_map/ppermute | solution.py:170
  127.5 4.3 %copy-start.9 = (f32[256,256]{1,0:T(8,128)S(1)}, f32[256,256]{1,0:T(8,128)}, u32[]{:S(2)}) copy-start(f32[256,256]{1,0:T(8,128)} %get-tuple-element.67) | copy-start | bytes 786436
  127.5 4.3 %copy-start.10 = (f32[256,256]{1,0:T(8,128)S(1)}, f32[256,256]{1,0:T(8,128)}, u32[]{:S(2)}) copy-start(f32[256,256]{1,0:T(8,128)} %get-tuple-element.68) | copy-start | bytes 786436
  127.7 62.9 %collective-permute-start.3 = (f32[2,2,256,256]{3,2,1,0:T(8,128)S(1)}, f32[2,2,256,256]{3,2,1,0:T(8,128)S(1)}, u32[]{:S(2)}, u32[]{:S(2)}) collective-permute-start(f32[2,2,256,256]{3,2,1,0:T(8,128)S(1)} %slice.133), channel_id=1, source_target_pairs={{0,1},{1,2},{2,3},{3,4},{4,5},{5,6},{6,7},{7,8},{8,9},{9,10},{10,1... | collective-permute-start | bytes 3145736 | tf_op jit(solution)/shard_map/ppermute | solution.py:170

commit v2 on v1

v2 whole, which is shorter than its diff:
```python
import functools
import math

import jax
import jax.numpy as jnp
import ml_dtypes
import numpy as np
from jax import lax
from jax.experimental import pallas as pl
from jax.experimental.pallas import tpu as pltpu
from jax.sharding import PartitionSpec as P

intensity_floor = 0.5
chirp_divisor = 2.0
WIDTH = 256
HALF = 128
ROWS, COLS = 64, 12
VMEM = pl.BlockSpec(memory_space=pltpu.VMEM)
f32, bf16 = jnp.float32, jnp.bfloat16


def right_form(matrix):
    return np.block([[matrix.real, matrix.imag], [-matrix.imag, matrix.real]])


def left_form(matrix):
    return np.block([[matrix.real, -matrix.imag], [matrix.imag, matrix.real]])


def in_two(block):
    high = block.astype(np.float32).astype(ml_dtypes.bfloat16)
    low = (block - high.astype(np.float64)).astype(np.float32).astype(ml_dtypes.bfloat16)
    return high, low


def for_right(block):
    high, low = in_two(block)
    return np.concatenate([high, high, low], axis=0)


def for_left(block):
    high, low = in_two(block)
    return np.concatenate([high, low, high], axis=1)


@functools.lru_cache
def tables():
    indices = np.arange(WIDTH)
    turns = (indices[:, None] * indices[None, :]) % WIDTH
    dft = np.exp(-2j * np.pi * turns / WIDTH) / np.sqrt(WIDTH)
    centered = np.where(indices < HALF, indices, indices - WIDTH).astype(np.float64)
    phase = np.exp(-1j * np.pi * centered**2 / (chirp_divisor * WIDTH))
    kernel = np.conj(dft) @ (phase[:, None] * dft)
    near, far = kernel[:HALF, :HALF], kernel[:HALF, HALF:]
    halves = [(near + far) / 2, (near - far) / 2]
    combs = [dft[:HALF, 0::2], dft[:HALF, 1::2]]
    forms = {
        "kernel_right": [for_right(right_form(m)) for m in halves],
        "kernel_left": [for_left(left_form(m)) for m in halves],
        "kernel_right_back": [for_right(left_form(m)) for m in halves],
        "kernel_left_back": [for_left(right_form(m)) for m in halves],
        "dft_right": [for_right(right_form(m)) for m in combs],
        "dft_left": [for_left(left_form(m.T)) for m in combs],
        "dft_right_back": [for_right(left_form(m.T)) for m in combs],
        "dft_left_back": [for_left(right_form(m)) for m in combs],
    }
    return {name: np.stack(pair) for name, pair in forms.items()}


def split(value):
    high = value.astype(bf16)
    return high, (value - high.astype(f32)).astype(bf16)


def times_right(field, table):
    high, low = split(field)
    return jnp.dot(jnp.concatenate([high, low, high], axis=1), table, preferred_element_type=f32)


def times_left(table, field):
    high, low = split(field)
    return jnp.dot(table, jnp.concatenate([high, high, low], axis=0), preferred_element_type=f32)


def both_sides(combs, right, left):
    turned = [times_right(combs[e], right[e]) for e in range(2)]
    out = []
    for e in range(2):
        slabs = []
        for mode in range(2):
            start = mode * WIDTH + e * HALF
            rows = [turned[k][start : start + HALF] for k in range(2)]
            top = jnp.concatenate([rows[0][:, :HALF], rows[1][:, :HALF]], axis=1)
            bottom = jnp.concatenate([rows[0][:, HALF:], rows[1][:, HALF:]], axis=1)
            slabs.append(jnp.concatenate([top, bottom], axis=0))
        out.append(times_left(left[e], jnp.concatenate(slabs, axis=1)))
    return out


def butterfly(plane):
    plane = jnp.concatenate([plane[:HALF] + plane[HALF:], plane[:HALF] - plane[HALF:]], axis=0)
    return plane[:, :HALF] + plane[:, HALF:], plane[:, :HALF] - plane[:, HALF:]


def fold(waves):
    parts = [(butterfly(re), butterfly(im)) for re, im in waves]
    return [
        jnp.concatenate([jnp.concatenate([re[e], im[e]], axis=1) for re, im in parts], axis=0) for e in range(2)
    ]


def comb_fields(fields):
    return [
        jnp.concatenate(
            [jnp.concatenate([part[:, e * HALF : (e + 1) * HALF] for part in pair], axis=1) for pair in fields], axis=0
        )
        for e in range(2)
    ]


def plane_of(out, mode, part):
    lanes = slice(mode * WIDTH, (mode + 1) * WIDTH)
    rows = slice(part * HALF, (part + 1) * HALF)
    return [out[e][rows, lanes] for e in range(2)]


def unfold(out):
    def spread(mode, part):
        even, odd = plane_of(out, mode, part)
        plane = jnp.concatenate([even + odd, even - odd], axis=0)
        even, odd = plane[:, :HALF], plane[:, HALF:]
        return jnp.concatenate([even + odd, even - odd], axis=1)

    return [(spread(mode, 0), spread(mode, 1)) for mode in range(2)]


def in_combs(out):
    return [tuple(jnp.concatenate(plane_of(out, mode, part), axis=0) for part in range(2)) for mode in range(2)]


def times(a, b):
    return a[0] * b[0] - a[1] * b[1], a[0] * b[1] + a[1] * b[0]


def times_conj(a, b):
    return a[0] * b[0] + a[1] * b[1], a[1] * b[0] - a[0] * b[1]


def iota(axis):
    return lax.broadcasted_iota(jnp.int32, (WIDTH, WIDTH), axis)


def one_hot(condition):
    return jnp.where(condition, 1.0, 0.0).astype(bf16)


def permute(left, planes, right):
    count = len(planes)
    high, low = split(jnp.concatenate(planes, axis=1))
    moved = jnp.dot(left, high, preferred_element_type=f32) + jnp.dot(left, low, preferred_element_type=f32)
    rows = jnp.concatenate([moved[:, k * WIDTH : (k + 1) * WIDTH] for k in range(count)], axis=0)
    high, low = split(rows)
    moved = jnp.dot(high, right, preferred_element_type=f32) + jnp.dot(low, right, preferred_element_type=f32)
    return [moved[k * WIDTH : (k + 1) * WIDTH] for k in range(count)]


MESH_ID = pl.DeviceIdType.MESH


def place():
    row = lax.axis_index("row")
    return row // 16, (row // 2) % 8, lax.axis_index("col"), row % 2


def device(x, y, z, core):
    return ((x * 8 + y) * 2 + core, z)


def start_copy(source, target, sent, landed, to):
    copy = pltpu.make_async_remote_copy(
        src_ref=source, dst_ref=target, send_sem=sent, recv_sem=landed, device_id=to, device_id_type=MESH_ID
    )
    copy.start()
    return copy


def wait_bytes(ref, semaphore):
    pltpu.make_async_copy(ref, ref, semaphore).wait()


class ProbeSum:
    def __init__(self, parts, total, from_core, near, from_x, mid, from_y, from_z, sent, landed, scale):
        self.parts, self.total, self.from_core, self.near = parts, total, from_core, near
        self.from_x, self.mid, self.from_y, self.from_z = from_x, mid, from_y, from_z
        self.sent, self.landed, self.scale = sent, landed, scale
        self.x, self.y, self.z, self.core = place()

    def x_peers(self):
        return [lax.rem(self.x + d, 4) for d in range(1, 4)]

    def y_peers(self):
        return [lax.rem(self.y + d, 8) for d in range(1, 8)]

    def z_peers(self):
        return [lax.rem(self.z + d, 12) for d in range(1, 12)]

    def columns(self, chunk):
        return chunk // 2, pl.ds(128 * (chunk % 2), 128)

    def stage(self, chunk, step):
        x, y, z, core = self.x, self.y, self.z, self.core
        mode, lanes = self.columns(chunk)
        other = device(x, y, z, 1 - core)
        sent, landed = self.sent.at[chunk, step], self.landed.at[chunk, step]
        arrived = self.landed.at[chunk, step - 1]
        mine = pl.ds(pl.multiple_of(64 * x + 8 * y, 8), 8)
        block = pl.ds(pl.multiple_of(64 * x, 64), 64)
        if step == 0:
            start_copy(self.parts.at[mode, 1 - core, :, lanes], self.from_core.at[chunk], sent, landed, other)
        elif step == 1:
            wait_bytes(self.from_core.at[chunk], arrived)
            self.near[chunk] = self.parts[mode, core, :, lanes] + self.from_core[chunk]
            for d, px in enumerate(self.x_peers()):
                rows = pl.ds(pl.multiple_of(64 * px, 64), 64)
                start_copy(self.near.at[chunk, rows], self.from_x.at[chunk, d], sent, landed, device(px, y, z, core))
        elif step == 2:
            wait_bytes(self.from_x.at[chunk], arrived)
            self.mid[chunk] = (self.near[chunk, block, :] + self.from_x[chunk, 0]) + (
                self.from_x[chunk, 1] + self.from_x[chunk, 2]
            )
            for d, py in enumerate(self.y_peers()):
                rows = pl.ds(pl.multiple_of(8 * py, 8), 8)
                start_copy(self.mid.at[chunk, rows], self.from_y.at[chunk, d], sent, landed, device(x, py, z, core))
        elif step == 3:
            wait_bytes(self.from_y.at[chunk], arrived)
            piece = self.mid[chunk, pl.ds(pl.multiple_of(8 * y, 8), 8), :]
            for d in range(7):
                piece = piece + self.from_y[chunk, d]
            self.from_z[chunk, z] = piece
            for pz in self.z_peers():
                start_copy(self.from_z.at[chunk, z], self.from_z.at[chunk, z], sent, landed, device(x, y, pz, core))
        elif step == 4:
            wait_bytes(self.from_z.at[chunk, pl.ds(0, 11)], arrived)
            piece = self.from_z[chunk, 0]
            for d in range(1, 12):
                piece = piece + self.from_z[chunk, d]
            self.total[mode, core, mine, lanes] = piece * self.scale
            spot = self.total.at[mode, core, mine, lanes]
            for py in self.y_peers():
                start_copy(spot, spot, sent, landed, device(x, py, z, core))
        elif step == 5:
            wait_bytes(self.total.at[mode, core, pl.ds(0, 56), lanes], arrived)
            spot = self.total.at[mode, core, block, lanes]
            for px in self.x_peers():
                start_copy(spot, spot, sent, landed, device(px, y, z, core))
        elif step == 6:
            wait_bytes(self.total.at[mode, core, pl.ds(0, 192), lanes], arrived)
            spot = self.total.at[mode, core, :, lanes]
            start_copy(spot, spot, sent, landed, other)
        elif step == 7:
            wait_bytes(self.total.at[mode, core, :, lanes], arrived)

    def drain(self, chunk):
        mode, lanes = self.columns(chunk)
        sizes = [
            self.from_core.at[chunk],
            self.from_x.at[chunk],
            self.from_y.at[chunk],
            self.from_z.at[chunk, pl.ds(0, 11)],
            self.total.at[mode, self.core, pl.ds(0, 56), lanes],
            self.total.at[mode, self.core, pl.ds(0, 192), lanes],
            self.total.at[mode, self.core, :, lanes],
        ]
        for step, ref in enumerate(sizes):
            wait_bytes(ref, self.sent.at[chunk, step])

    def greet(self, barrier):
        x, y, z, core = self.x, self.y, self.z, self.core
        peers = [device(x, y, z, 1 - core)]
        peers += [device(px, y, z, core) for px in self.x_peers()]
        peers += [device(x, py, z, core) for py in self.y_peers()]
        peers += [device(x, y, pz, core) for pz in self.z_peers()]
        for peer in peers:
            pl.semaphore_signal(barrier, inc=1, device_id=peer, device_id_type=MESH_ID)
        return len(peers)


PROBE_SUM_SCRATCH = [
    pltpu.VMEM((4, 256, 128), jnp.float32),
    pltpu.VMEM((4, 256, 128), jnp.float32),
    pltpu.VMEM((4, 3, 64, 128), jnp.float32),
    pltpu.VMEM((4, 64, 128), jnp.float32),
    pltpu.VMEM((4, 7, 8, 128), jnp.float32),
    pltpu.VMEM((4, 12, 8, 128), jnp.float32),
    pltpu.SemaphoreType.DMA((4, 7)),
    pltpu.SemaphoreType.DMA((4, 7)),
]


def halo_kernel(
    tile, probe, corner, amplitude, kernel_right, kernel_left,
    patch, moved_probe, wave, spectrum, corners,
    below, merged, side, left_corner, own_spectrum, side_spectrum, sent, landed,
):
    row, z = lax.axis_index("row"), lax.axis_index("col")
    core = lax.rem(row, 2)
    up, down = (lax.rem(row + ROWS - 1, ROWS), z), (lax.rem(row + 1, ROWS), z)
    right, left = (row, lax.rem(z + 1, COLS)), (row, lax.rem(z + COLS - 1, COLS))
    onward = (row, lax.rem(z + COLS - 1 + 2 * core, COLS))
    barrier = pltpu.get_barrier_semaphore()
    for peer in (up, down, right, left):
        pl.semaphore_signal(barrier, inc=1, device_id=peer, device_id_type=MESH_ID)

    rows, lanes = iota(0), iota(1)
    to_combs = one_hot(lanes == 2 * lax.rem(rows, HALF) + rows // HALF)
    from_combs = one_hot(rows == 2 * lax.rem(lanes, HALF) + lanes // HALF)
    own_spectrum[...] = permute(to_combs, [amplitude[...]], from_combs)[0]
    pl.semaphore_wait(barrier, 4)

    def chunk(index):
        layer, part, half = index // 4, (index // 2) % 2, index % 2
        return layer, part, pl.ds(half * HALF, HALF)

    copies = [start_copy(corner, left_corner, sent.at[16], landed.at[16], right)]
    for index in range(8):
        spot = chunk(index)
        copies.append(start_copy(tile.at[spot], below.at[spot], sent.at[index], landed.at[index], up))

    @pl.when(core == 1)
    def _():
        start_copy(own_spectrum, side_spectrum, sent.at[17], landed.at[17], right)

    wait_bytes(left_corner, landed.at[16])
    own, other = corner[...], left_corner[...]
    working = own + core * (other - own)
    handing = other + core * (own - other)
    row_start, col_start = working[0:1, :], working[1:2, :]
    hand_start = handing[0:1, :]
    corners[0] = working
    corners[1] = handing

    for index in range(8):
        layer, part, span = chunk(index)
        wait_bytes(below.at[layer, part, span], landed.at[index])
        mine, under = tile[layer, part, span, :], below[layer, part, span, :]
        merged[layer, part, span, :] = jnp.where(rows[span.start : span.start + HALF] >= hand_start, mine, under)
        spot = merged.at[layer, part, span]
        copies.append(start_copy(spot, side.at[layer, part, span], sent.at[8 + index], landed.at[8 + index], onward))
        patch[layer, part, span, :] = jnp.where(rows[span.start : span.start + HALF] >= row_start, mine, under)
        if index == 3:
            shift_rows = one_hot(jnp.bitwise_and(rows - lanes - row_start, WIDTH - 1) == 0)
            shift_cols = one_hot(jnp.bitwise_and(lanes - rows - col_start, WIDTH - 1) == 0)
            planes = [probe[mode, part] for mode in range(2) for part in range(2)]
            for k, plane in enumerate(permute(shift_rows, planes, shift_cols)):
                moved_probe[k // 2, k % 2] = plane

    own_columns = jnp.where(lanes >= col_start, 1, 0) != core

    def finish(layer):
        for index in range(4):
            wait_bytes(side.at[chunk(4 * layer + index)], landed.at[8 + 4 * layer + index])
        for part in range(2):
            patch[layer, part] = jnp.where(own_columns, patch[layer, part], side[layer, part])

    finish(0)
    first = (patch[0, 0], patch[0, 1])
    waves = [times((moved_probe[mode, 0], moved_probe[mode, 1]), first) for mode in range(2)]
    for mode, pair in enumerate(unfold(both_sides(fold(waves), kernel_right, kernel_left))):
        for part in range(2):
            wave[mode, part] = pair[part]
    finish(1)

    @pl.when(core == 0)
    def _():
        spectrum[...] = own_spectrum[...]

    @pl.when(core == 1)
    def _():
        wait_bytes(side_spectrum, landed.at[17])
        spectrum[...] = side_spectrum[...]
        wait_bytes(side_spectrum, sent.at[17])

    for copy in copies:
        copy.wait_send()


def halo_in(tile, probe, corner, amplitude, names):
    shape = lambda *dims: jax.ShapeDtypeStruct(dims, f32)
    full = (2, 2, WIDTH, WIDTH)
    return pl.pallas_call(
        halo_kernel,
        out_shape=[
            shape(*full), shape(*full), shape(*full), shape(WIDTH, WIDTH), jax.ShapeDtypeStruct((2, 8, WIDTH), jnp.int32),
        ],
        in_specs=[VMEM] * 6,
        out_specs=[VMEM] * 5,
        scratch_shapes=[
            pltpu.VMEM(full, f32),
            pltpu.VMEM(full, f32),
            pltpu.VMEM(full, f32),
            pltpu.VMEM((8, WIDTH), jnp.int32),
            pltpu.VMEM((WIDTH, WIDTH), f32),
            pltpu.VMEM((WIDTH, WIDTH), f32),
            pltpu.SemaphoreType.DMA((18,)),
            pltpu.SemaphoreType.DMA((18,)),
        ],
        compiler_params=pltpu.CompilerParams(collective_id=1, has_side_effects=True, vmem_limit_bytes=48 << 20),
    )(tile, probe, corner, amplitude, names["kernel_right"], names["kernel_left"])


def gradient_kernel(
    patch, moved_probe, wave, spectrum, corners,
    dft_right, dft_left, dft_right_back, dft_left_back, kernel_right_back, kernel_left_back,
    object_gradient, total,
    parts, side_out, side_in, down_out, down_in, grads, sent, landed, *scratch,
):
    probe_total = ProbeSum(parts, total, *scratch, 1.0 / math.sqrt(ROWS * COLS))
    row, z = lax.axis_index("row"), lax.axis_index("col")
    core = lax.rem(row, 2)
    up, down = (lax.rem(row + ROWS - 1, ROWS), z), (lax.rem(row + 1, ROWS), z)
    back = (row, lax.rem(z + 1 + (COLS - 2) * core, COLS))
    barrier = pltpu.get_barrier_semaphore()
    count = probe_total.greet(barrier)
    for peer in (up, down):
        pl.semaphore_signal(barrier, inc=1, device_id=peer, device_id_type=MESH_ID)

    rows, lanes = iota(0), iota(1)
    row_start, col_start, hand_start = corners[0, 0:1, :], corners[0, 1:2, :], corners[1, 0:1, :]
    own_columns = jnp.where(lanes >= col_start, 1, 0) != core
    second = (patch[1, 0], patch[1, 1])
    waves = [(wave[mode, 0], wave[mode, 1]) for mode in range(2)]
    passed = [times(pair, second) for pair in waves]
    far = in_combs(both_sides(fold(passed), dft_right, dft_left))
    intensity = far[0][0] * far[0][0] + far[0][1] * far[0][1] + (far[1][0] * far[1][0] + far[1][1] * far[1][1])
    weight = 2.0 - 2.0 * spectrum[...] * lax.rsqrt(intensity + intensity_floor)
    far = [(weight * re, weight * im) for re, im in far]
    slope = unfold(both_sides(comb_fields(far), dft_right_back, dft_left_back))
    pl.semaphore_wait(barrier, count + 2)
    copies = []

    def send_side(layer, terms):
        for part in range(2):
            grads[layer, part] = terms[0][part] + terms[1][part]
            side_out[layer, part] = jnp.where(own_columns, 0.0, grads[layer, part])
        copies.append(start_copy(side_out.at[layer], side_in.at[layer], sent.at[layer], landed.at[layer], back))

    def send_down(layer):
        wait_bytes(side_in.at[layer], landed.at[layer])
        for part in range(2):
            mine = jnp.where(own_columns, grads[layer, part], 0.0)
            other = side_in[layer, part]
            down_out[layer, part] = jnp.where(rows < row_start, mine, 0.0) + jnp.where(rows < hand_start, other, 0.0)
            grads[layer, part] = jnp.where(rows < row_start, 0.0, mine) + jnp.where(rows < hand_start, 0.0, other)
        copies.append(start_copy(down_out.at[layer], down_in.at[layer], sent.at[2 + layer], landed.at[2 + layer], down))

    def finish(layer):
        wait_bytes(down_in.at[layer], landed.at[2 + layer])
        object_gradient[layer] = grads[layer] + down_in[layer]

    send_side(1, [times_conj(slope[mode], waves[mode]) for mode in range(2)])
    slope = [times_conj(pair, second) for pair in slope]
    slope = unfold(both_sides(fold(slope), kernel_right_back, kernel_left_back))
    first = (patch[0, 0], patch[0, 1])
    shift_rows = one_hot(jnp.bitwise_and(lanes - rows - row_start, WIDTH - 1) == 0)
    shift_cols = one_hot(jnp.bitwise_and(rows - lanes - col_start, WIDTH - 1) == 0)
    for mode in range(2):
        for part, plane in enumerate(permute(shift_rows, list(times_conj(slope[mode], first)), shift_cols)):
            parts[mode, part] = plane
        for chunk in range(2):
            probe_total.stage(2 * mode + chunk, 0)
    send_side(0, [times_conj(slope[mode], (moved_probe[mode, 0], moved_probe[mode, 1])) for mode in range(2)])
    for step in range(1, 8):
        for chunk in range(4):
            probe_total.stage(chunk, step)
        if step == 2:
            send_down(1)
        if step == 3:
            send_down(0)
        if step == 5:
            finish(1)
        if step == 6:
            finish(0)
    for chunk in range(4):
        probe_total.drain(chunk)
    for copy in copies:
        copy.wait_send()


def gradients(patch, moved_probe, wave, spectrum, corners, names):
    full = (2, 2, WIDTH, WIDTH)
    return pl.pallas_call(
        gradient_kernel,
        out_shape=[jax.ShapeDtypeStruct(full, f32)] * 2,
        in_specs=[VMEM] * 11,
        out_specs=[VMEM] * 2,
        scratch_shapes=[pltpu.VMEM(full, f32)] * 6
        + [pltpu.SemaphoreType.DMA((4,)), pltpu.SemaphoreType.DMA((4,))]
        + PROBE_SUM_SCRATCH,
        compiler_params=pltpu.CompilerParams(collective_id=2, has_side_effects=True, vmem_limit_bytes=48 << 20),
    )(
        patch, moved_probe, wave, spectrum, corners,
        names["dft_right"], names["dft_left"], names["dft_right_back"], names["dft_left_back"],
        names["kernel_right_back"], names["kernel_left_back"],
    )


def on_device(object_field, probe, scan_positions, amplitudes):
    names = {name: jnp.asarray(table) for name, table in tables().items()}
    tile_rows, tile_cols = object_field.shape[2:]
    base = jnp.stack([lax.axis_index("row") * tile_rows, lax.axis_index("col") * tile_cols])
    corner = scan_positions[0, 0, 0] - base
    corner = jnp.broadcast_to(jnp.pad(corner, (0, 6))[:, None], (8, WIDTH))
    held = halo_in(object_field, probe, corner, amplitudes[0, 0, 0], names)
    return tuple(gradients(*held, names))


def solution(mesh):
    in_specs = (
        P(None, None, "row", "col"),
        P(),
        P("row", "col", None, None),
        P("row", "col", None, None, None),
    )
    out_specs = (P(None, None, "row", "col"), P())
    return jax.shard_map(
        on_device, mesh=mesh, in_specs=in_specs, out_specs=out_specs, check_vma=False
    )
```

time: 194 us -> 93.4 us (0.48)
  waiting for transfers between devices: 48.8 us -> 0 us
  matrix products: 24.7 us -> 0 us
  Pallas kernels: 58.4 us -> 81.7 us
  starting transfers between devices: 19.4 us -> 0 us
  local copies, waits for them, and re-layouts: 28.1 us -> 10.6 us
  other arithmetic: 10.8 us -> 0.08 us
    ppermute x4 -> x0, waiting for transfers between devices: 48.8 us -> none  [from_behind(): return lax.ppermute(array, axis, pairs)]
    dot_general x12 -> x0, matrix products: 24.7 us -> none  [the longest x4 9.65 us: apply_both(): return jnp.einsum('mtab,tbsc->msac', field, right_block, precision=highest)]
    pallas_call x1 -> x2, Pallas kernels: 58.4 us -> 81.7 us  [the longest x1 47.7 us: gradients(): pl.pallas_call(gradient_kernel, out_shape=[jax.ShapeDtypeStruct(full, f32...]
    ppermute x4 -> x0, starting transfers between devices: 19.4 us -> none  [from_behind(): return lax.ppermute(array, axis, pairs)]
    dynamic_update_slice x1 -> x0, local copies, waits for them, and re-layouts: 11.8 us -> none  [on_device(): lax.dynamic_update_slice(object_grads, patch_part, corner_start)]
    unnamed x33 -> x30, local copies, waits for them, and re-layouts: 5.55 us -> 10.5 us
    mul x3 -> x0, local copies, waits for them, and re-layouts: 3.9 us -> none  [complex_times(): out_real = field[:, 0] * factor[0] - field[:, 1] * factor[1]]
    slice x3 -> x0, local copies, waits for them, and re-layouts: 3.38 us -> none  [the longest x1 1.96 us: on_device(): from_above = from_behind(object_grads[:, :, tile_rows:, :], 'row', 1)]
  transfers between devices with their start and end apart: 4 -> 0, of which waited for: 3 -> 0; matrix products, arithmetic and copies ran while one was open for 8% -> 0% of each run, Pallas kernels for 30% -> 0%
where the time goes in v2:
time: 93.4 us; the launch traced here: 93 us
  Pallas kernels  81.7 us (87%)
  local copies, waits for them, and re-layouts  10.6 us (11%)
    pallas_call x1, Pallas kernels, gradients(): pl.pallas_call(gradient_kernel, out_shape=[jax.ShapeDtypeStruct(full, f32...  47.7 us
    pallas_call x1, Pallas kernels, halo_in(): pl.pallas_call(halo_kernel, out_shape=[shape(*full), shape(*full), shape(...  33.9 us
    unnamed x30, local copies, waits for them, and re-layouts  10.5 us

profile of v2, /device:TPU:1, one launch (start us, length us, event | category | flops | bytes accessed | tf_op | source)
XLA Modules:
  0.0 93.0 jit_solution(4997033672966710648)
XLA Ops:
  0.6 0.0 copy-start.13
  0.7 0.6 copy-done.13
  1.3 0.1 add_subtract_fusion
  1.4 0.1 broadcast_in_dim.2.corner
  1.5 1.1 %copy-done.3 = bf16[2,256,768]{2,1,0:T(8,128)(2,1)S(1)} copy-done((bf16[2,256,768]{2,1,0:T(8,128)(2,1)S(1)}, bf16[2,256,768]{2,1,0:T(8,128)(2,1)}, u32[]{:S(2)}) %copy-start.3) | copy-done | bytes 786456
  2.6 1.1 %copy-done.4 = bf16[2,768,256]{2,1,0:T(8,128)(2,1)S(1)} copy-done((bf16[2,768,256]{2,1,0:T(8,128)(2,1)S(1)}, bf16[2,768,256]{2,1,0:T(8,128)(2,1)}, u32[]{:S(2)}) %copy-start.4) | copy-done | bytes 786456
  3.7 0.9 %copy-done.11 = f32[1,1,1,256,256]{4,3,2,1,0:T(8,128)S(1)} copy-done((f32[1,1,1,256,256]{4,3,2,1,0:T(8,128)S(1)}, f32[1,1,1,256,256]{4,3,2,1,0:T(8,128)}, u32[]{:S(2)}) %copy-start.11) | copy-done | bytes 262168
  4.7 0.0 copy-start.9
  4.7 33.9 %shard_map.131 = (f32[2,2,256,256]{3,2,1,0:T(8,128)S(1)}, f32[2,2,256,256]{3,2,1,0:T(8,128)S(1)}, f32[2,2,256,256]{3,2,1,0:T(8,128)S(1)}, f32[256,256]{1,0:T(8,128)S(1)}, s32[2,8,256]{2,1,0:T(8,128)S(1)}) custom-call(f32[2,2,256,256]{3,2,1,0:T(8,128)} %tile.1, f32[2,2,256,256]{3,2,1,0:T(8,128)} %probe.1, s32[8,256]{1,0:T(8,128)S(1)} %broadcast_in_dim.2.corner, ...), custom_call_target="tpu_custom_call" | custom-call | tf_op jit(solution)/shard_map/pallas_call | solution.py:390
  38.6 0.0 copy-start
  38.6 1.0 %copy-done = f32[2,2,256,256]{3,2,1,0:T(8,128)} copy-done((f32[2,2,256,256]{3,2,1,0:T(8,128)}, f32[2,2,256,256]{3,2,1,0:T(8,128)S(1)}, u32[]{:S(2)}) %copy-start) | copy-done | bytes 1048600
  39.6 1.0 %copy-done.1 = f32[2,2,256,256]{3,2,1,0:T(8,128)} copy-done((f32[2,2,256,256]{3,2,1,0:T(8,128)}, f32[2,2,256,256]{3,2,1,0:T(8,128)S(1)}, u32[]{:S(2)}) %copy-start.1) | copy-done | bytes 1048600
  40.6 1.0 %copy-done.2 = f32[2,2,256,256]{3,2,1,0:T(8,128)} copy-done((f32[2,2,256,256]{3,2,1,0:T(8,128)}, f32[2,2,256,256]{3,2,1,0:T(8,128)S(1)}, u32[]{:S(2)}) %copy-start.2) | copy-done | bytes 1048600
  41.6 0.0 copy-done.5
  41.6 0.0 copy-done.6
  41.6 0.0 copy-done.7
  41.6 0.0 copy-done.8
  41.6 0.0 copy-done.9
  41.6 0.0 copy-start.10
  41.6 1.1 %copy-done.10 = bf16[2,768,256]{2,1,0:T(8,128)(2,1)S(1)} copy-done((bf16[2,768,256]{2,1,0:T(8,128)(2,1)S(1)}, bf16[2,768,256]{2,1,0:T(8,128)(2,1)}, u32[]{:S(2)}) %copy-start.10) | copy-done | bytes 786456
  42.7 47.7 %shard_map.132 = (f32[2,2,256,256]{3,2,1,0:T(8,128)S(1)}, f32[2,2,256,256]{3,2,1,0:T(8,128)}) custom-call(f32[2,2,256,256]{3,2,1,0:T(8,128)} %copy-done, f32[2,2,256,256]{3,2,1,0:T(8,128)} %copy-done.1, f32[2,2,256,256]{3,2,1,0:T(8,128)} %copy-done.2, f32[256,256]{1,0:T(8,128)S(1)} %get-tuple-element.10.spectrum, ...), custom_call_target="tpu_custom_call" | custom-call | tf_op jit(solution)/shard_map/pallas_call | solution.py:491
  90.5 1.0 %copy.16 = f32[2,2,256,256]{3,2,1,0:T(8,128)} copy(f32[2,2,256,256]{3,2,1,0:T(8,128)S(1)} %get-tuple-element.14) | data formatting | bytes 2097152
  91.4 0.6 copy-done.12
  92.1 1.0 %copy.17 = f32[2,2,256,256]{3,2,1,0:T(8,128)} copy(f32[2,2,256,256]{3,2,1,0:T(8,128)S(1)} %copy-done.12) | data formatting | bytes 2097152
  (11 shorter events, 0.0 us)
Async XLA Ops:
  0.6 0.7 copy-start.13
  1.5 1.1 %copy-start.3 = (bf16[2,256,768]{2,1,0:T(8,128)(2,1)S(1)}, bf16[2,256,768]{2,1,0:T(8,128)(2,1)}, u32[]{:S(2)}) copy-start(bf16[2,256,768]{2,1,0:T(8,128)(2,1)} %constant.27.clone.kernel_left) | copy-start | bytes 2359300
  2.6 1.1 %copy-start.4 = (bf16[2,768,256]{2,1,0:T(8,128)(2,1)S(1)}, bf16[2,768,256]{2,1,0:T(8,128)(2,1)}, u32[]{:S(2)}) copy-start(bf16[2,768,256]{2,1,0:T(8,128)(2,1)} %constant.26.clone.kernel_right) | copy-start | bytes 2359300
  3.7 0.9 %copy-start.11 = (f32[1,1,1,256,256]{4,3,2,1,0:T(8,128)S(1)}, f32[1,1,1,256,256]{4,3,2,1,0:T(8,128)}, u32[]{:S(2)}) copy-start(f32[1,1,1,256,256]{4,3,2,1,0:T(8,128)} %param.15) | copy-start | bytes 786436
  4.7 36.9 %copy-start.5 = (bf16[2,256,768]{2,1,0:T(8,128)(2,1)S(1)}, bf16[2,256,768]{2,1,0:T(8,128)(2,1)}, u32[]{:S(2)}) copy-start(bf16[2,256,768]{2,1,0:T(8,128)(2,1)} %constant.33.clone.dft_left_back) | copy-start | bytes 2359300
  4.7 36.9 %copy-start.6 = (bf16[2,768,256]{2,1,0:T(8,128)(2,1)S(1)}, bf16[2,768,256]{2,1,0:T(8,128)(2,1)}, u32[]{:S(2)}) copy-start(bf16[2,768,256]{2,1,0:T(8,128)(2,1)} %constant.32.clone.dft_right_back) | copy-start | bytes 2359300
  4.7 36.9 %copy-start.7 = (bf16[2,256,768]{2,1,0:T(8,128)(2,1)S(1)}, bf16[2,256,768]{2,1,0:T(8,128)(2,1)}, u32[]{:S(2)}) copy-start(bf16[2,256,768]{2,1,0:T(8,128)(2,1)} %constant.31.clone.dft_left) | copy-start | bytes 2359300
  4.7 36.9 %copy-start.8 = (bf16[2,768,256]{2,1,0:T(8,128)(2,1)S(1)}, bf16[2,768,256]{2,1,0:T(8,128)(2,1)}, u32[]{:S(2)}) copy-start(bf16[2,768,256]{2,1,0:T(8,128)(2,1)} %constant.30.clone.dft_right) | copy-start | bytes 2359300
  4.7 36.9 %copy-start.9 = (bf16[2,256,768]{2,1,0:T(8,128)(2,1)S(1)}, bf16[2,256,768]{2,1,0:T(8,128)(2,1)}, u32[]{:S(2)}) copy-start(bf16[2,256,768]{2,1,0:T(8,128)(2,1)} %constant.29.clone.kernel_left_back) | copy-start | bytes 2359300
  38.6 1.0 %copy-start = (f32[2,2,256,256]{3,2,1,0:T(8,128)}, f32[2,2,256,256]{3,2,1,0:T(8,128)S(1)}, u32[]{:S(2)}) copy-start(f32[2,2,256,256]{3,2,1,0:T(8,128)S(1)} %get-tuple-element.7.patch) | copy-start | bytes 3145732
  39.6 1.0 %copy-start.1 = (f32[2,2,256,256]{3,2,1,0:T(8,128)}, f32[2,2,256,256]{3,2,1,0:T(8,128)S(1)}, u32[]{:S(2)}) copy-start(f32[2,2,256,256]{3,2,1,0:T(8,128)S(1)} %get-tuple-element.8.moved_probe) | copy-start | bytes 3145732
  40.6 1.0 %copy-start.2 = (f32[2,2,256,256]{3,2,1,0:T(8,128)}, f32[2,2,256,256]{3,2,1,0:T(8,128)S(1)}, u32[]{:S(2)}) copy-start(f32[2,2,256,256]{3,2,1,0:T(8,128)S(1)} %get-tuple-element.9.wave) | copy-start | bytes 3145732
  41.6 1.1 %copy-start.10 = (bf16[2,768,256]{2,1,0:T(8,128)(2,1)S(1)}, bf16[2,768,256]{2,1,0:T(8,128)(2,1)}, u32[]{:S(2)}) copy-start(bf16[2,768,256]{2,1,0:T(8,128)(2,1)} %constant.28.clone.kernel_right_back) | copy-start | bytes 2359300
  90.5 1.6 %copy-start.12 = (f32[2,2,256,256]{3,2,1,0:T(8,128)S(1)}, f32[2,2,256,256]{3,2,1,0:T(8,128)}, u32[]{:S(2)}) copy-start(f32[2,2,256,256]{3,2,1,0:T(8,128)} %get-tuple-element.15) | copy-start | bytes 3145732

commit v3 on v2

v3 whole, which is shorter than its diff:
```python
import functools
import math

import jax
import jax.numpy as jnp
import ml_dtypes
import numpy as np
from jax import lax
from jax.experimental import pallas as pl
from jax.experimental.pallas import tpu as pltpu
from jax.sharding import PartitionSpec as P

intensity_floor = 0.5
chirp_divisor = 2.0
WIDTH = 256
HALF = 128
ROWS, COLS = 64, 12
f32, bf16 = jnp.float32, jnp.bfloat16


def right_form(matrix):
    return np.block([[matrix.real, matrix.imag], [-matrix.imag, matrix.real]])


def left_form(matrix):
    return np.block([[matrix.real, -matrix.imag], [matrix.imag, matrix.real]])


@functools.lru_cache
def tables():
    indices = np.arange(WIDTH)
    turns = (indices[:, None] * indices[None, :]) % WIDTH
    dft = np.exp(-2j * np.pi * turns / WIDTH) / np.sqrt(WIDTH)
    centered = np.where(indices < HALF, indices, indices - WIDTH).astype(np.float64)
    phase = np.exp(-1j * np.pi * centered**2 / (chirp_divisor * WIDTH))
    kernel = np.conj(dft) @ (phase[:, None] * dft)
    near, far = kernel[:HALF, :HALF], kernel[:HALF, HALF:]
    halves = [(near + far) / 2, (near - far) / 2]
    combs = [dft[:HALF, 0::2], dft[:HALF, 1::2]]
    blocks = np.stack(
        [
            [right_form(m) for m in halves],
            [left_form(m) for m in halves],
            [right_form(m) for m in combs],
            [left_form(m.T) for m in combs],
        ]
    )
    high = blocks.astype(np.float32).astype(ml_dtypes.bfloat16)
    low = (blocks - high.astype(np.float64)).astype(np.float32).astype(ml_dtypes.bfloat16)
    return np.stack([high, low], axis=2)


KERNEL, KERNEL_BACK, DFT, DFT_BACK = (0, 1), (1, 0), (2, 3), (3, 2)


def split(value):
    high = value.astype(bf16)
    return high, (value - high.astype(f32)).astype(bf16)


def times_right(field, table):
    high, low = split(field)
    blocks = jnp.concatenate([table[0], table[0], table[1]], axis=0)
    return jnp.dot(jnp.concatenate([high, low, high], axis=1), blocks, preferred_element_type=f32)


def times_left(table, field):
    high, low = split(field)
    blocks = jnp.concatenate([table[0], table[1], table[0]], axis=1)
    return jnp.dot(blocks, jnp.concatenate([high, high, low], axis=0), preferred_element_type=f32)


def both_sides(combs, table, sides):
    right, left = sides
    turned = [times_right(combs[e], table[right, e]) for e in range(2)]
    out = []
    for e in range(2):
        slabs = []
        for start in range(e * HALF, combs[0].shape[0], WIDTH):
            rows = [turned[k][start : start + HALF] for k in range(2)]
            top = jnp.concatenate([rows[0][:, :HALF], rows[1][:, :HALF]], axis=1)
            bottom = jnp.concatenate([rows[0][:, HALF:], rows[1][:, HALF:]], axis=1)
            slabs.append(jnp.concatenate([top, bottom], axis=0))
        out.append(times_left(table[left, e], jnp.concatenate(slabs, axis=1)))
    return out


def butterfly(plane):
    plane = jnp.concatenate([plane[:HALF] + plane[HALF:], plane[:HALF] - plane[HALF:]], axis=0)
    return plane[:, :HALF] + plane[:, HALF:], plane[:, :HALF] - plane[:, HALF:]


def fold(waves):
    parts = [(butterfly(re), butterfly(im)) for re, im in waves]
    return [
        jnp.concatenate([jnp.concatenate([re[e], im[e]], axis=1) for re, im in parts], axis=0) for e in range(2)
    ]


def comb_fields(fields):
    return [
        jnp.concatenate(
            [jnp.concatenate([part[:, e * HALF : (e + 1) * HALF] for part in pair], axis=1) for pair in fields], axis=0
        )
        for e in range(2)
    ]


def plane_of(out, mode, part):
    lanes = slice(mode * WIDTH, (mode + 1) * WIDTH)
    rows = slice(part * HALF, (part + 1) * HALF)
    return [out[e][rows, lanes] for e in range(2)]


def unfold(out):
    def spread(mode, part):
        even, odd = plane_of(out, mode, part)
        plane = jnp.concatenate([even + odd, even - odd], axis=0)
        even, odd = plane[:, :HALF], plane[:, HALF:]
        return jnp.concatenate([even + odd, even - odd], axis=1)

    return [(spread(mode, 0), spread(mode, 1)) for mode in range(out[0].shape[1] // WIDTH)]


def in_combs(out):
    return [tuple(jnp.concatenate(plane_of(out, mode, part), axis=0) for part in range(2)) for mode in range(2)]


def times(a, b):
    return a[0] * b[0] - a[1] * b[1], a[0] * b[1] + a[1] * b[0]


def times_conj(a, b):
    return a[0] * b[0] + a[1] * b[1], a[1] * b[0] - a[0] * b[1]


def iota(axis):
    return lax.broadcasted_iota(jnp.int32, (WIDTH, WIDTH), axis)


def one_hot(condition):
    return jnp.where(condition, 1.0, 0.0).astype(bf16)


def permute(left, planes, right):
    count = len(planes)
    high, low = split(jnp.concatenate(planes, axis=1))
    moved = jnp.dot(left, high, preferred_element_type=f32) + jnp.dot(left, low, preferred_element_type=f32)
    rows = jnp.concatenate([moved[:, k * WIDTH : (k + 1) * WIDTH] for k in range(count)], axis=0)
    high, low = split(rows)
    moved = jnp.dot(high, right, preferred_element_type=f32) + jnp.dot(low, right, preferred_element_type=f32)
    return [moved[k * WIDTH : (k + 1) * WIDTH] for k in range(count)]


MESH_ID = pl.DeviceIdType.MESH


def place():
    row = lax.axis_index("row")
    return row // 16, (row // 2) % 8, lax.axis_index("col"), row % 2


def device(x, y, z, core):
    return ((x * 8 + y) * 2 + core, z)


def start_copy(source, target, sent, landed, to):
    copy = pltpu.make_async_remote_copy(
        src_ref=source, dst_ref=target, send_sem=sent, recv_sem=landed, device_id=to, device_id_type=MESH_ID
    )
    copy.start()
    return copy


def wait_bytes(ref, semaphore):
    pltpu.make_async_copy(ref, ref, semaphore).wait()


class ProbeSum:
    GRAIN = (4, 4, 4, 4, 4, 4, 4, 4)

    def __init__(self, parts, total, from_core, near, from_x, mid, from_y, from_z, sent, landed):
        self.parts, self.total, self.from_core, self.near = parts, total, from_core, near
        self.from_x, self.mid, self.from_y, self.from_z = from_x, mid, from_y, from_z
        self.sent, self.landed = sent, landed
        self.x, self.y, self.z, self.core = place()
        self.arrived = set()

    def x_peers(self):
        return [lax.rem(self.x + d, 4) for d in range(1, 4)]

    def y_peers(self):
        return [lax.rem(self.y + d, 8) for d in range(1, 8)]

    def z_peers(self):
        return [lax.rem(self.z + d, 12) for d in range(1, 12)]

    def cut(self, step, unit):
        grain = self.GRAIN[step]
        if grain == 1:
            return slice(0, 2), slice(0, 256)
        if grain == 2:
            return slice(unit, unit + 1), slice(0, 256)
        return slice(unit // 2, unit // 2 + 1), slice(128 * (unit % 2), 128 * (unit % 2) + 128)

    def volume(self, step, unit):
        modes, lanes = self.cut(step, unit)
        modes, lanes = pl.ds(modes.start, modes.stop - modes.start), pl.ds(lanes.start, lanes.stop - lanes.start)
        if step == 0:
            return self.from_core.at[modes, :, lanes]
        if step == 1:
            return self.from_x.at[:, modes, :, lanes]
        if step == 2:
            return self.from_y.at[:, modes, :, lanes]
        if step == 3:
            return self.from_z.at[pl.ds(0, 11), modes, :, lanes]
        rows = {4: 56, 5: 192, 6: 256}[step]
        return self.total.at[modes, self.core, pl.ds(0, rows), lanes]

    def await_step(self, step, modes, lanes):
        for unit in range(self.GRAIN[step]):
            m, l = self.cut(step, unit)
            apart = m.stop <= modes.start or modes.stop <= m.start or l.stop <= lanes.start or lanes.stop <= l.start
            if not apart and (step, unit) not in self.arrived:
                self.arrived.add((step, unit))
                wait_bytes(self.volume(step, unit), self.landed.at[step, unit])

    def stage(self, step, unit):
        x, y, z, core = self.x, self.y, self.z, self.core
        modes, lanes = self.cut(step, unit)
        if step > 0:
            self.await_step(step - 1, modes, lanes)
        if step == 7:
            return
        m, l = pl.ds(modes.start, modes.stop - modes.start), pl.ds(lanes.start, lanes.stop - lanes.start)
        sent, landed = self.sent.at[step, unit], self.landed.at[step, unit]
        other = device(x, y, z, 1 - core)
        mine = pl.ds(pl.multiple_of(64 * x + 8 * y, 8), 8)
        block = pl.ds(pl.multiple_of(64 * x, 64), 64)
        if step == 0:
            start_copy(self.parts.at[m, 1 - core, :, l], self.from_core.at[m, :, l], sent, landed, other)
        elif step == 1:
            self.near[m, :, l] = self.parts[m, core, :, l] + self.from_core[m, :, l]
            for d, px in enumerate(self.x_peers()):
                rows = pl.ds(pl.multiple_of(64 * px, 64), 64)
                start_copy(self.near.at[m, rows, l], self.from_x.at[d, m, :, l], sent, landed, device(px, y, z, core))
        elif step == 2:
            self.mid[m, :, l] = (self.near[m, block, l] + self.from_x[0, m, :, l]) + (
                self.from_x[1, m, :, l] + self.from_x[2, m, :, l]
            )
            for d, py in enumerate(self.y_peers()):
                rows = pl.ds(pl.multiple_of(8 * py, 8), 8)
                start_copy(self.mid.at[m, rows, l], self.from_y.at[d, m, :, l], sent, landed, device(x, py, z, core))
        elif step == 3:
            piece = self.mid[m, pl.ds(pl.multiple_of(8 * y, 8), 8), l]
            for d in range(7):
                piece = piece + self.from_y[d, m, :, l]
            self.from_z[z, m, :, l] = piece
            spot = self.from_z.at[z, m, :, l]
            for pz in self.z_peers():
                start_copy(spot, spot, sent, landed, device(x, y, pz, core))
        elif step == 4:
            piece = self.from_z[0, m, :, l]
            for d in range(1, 12):
                piece = piece + self.from_z[d, m, :, l]
            self.total[m, core, mine, l] = piece
            spot = self.total.at[m, core, mine, l]
            for py in self.y_peers():
                start_copy(spot, spot, sent, landed, device(x, py, z, core))
        elif step == 5:
            spot = self.total.at[m, core, block, l]
            for px in self.x_peers():
                start_copy(spot, spot, sent, landed, device(px, y, z, core))
        elif step == 6:
            spot = self.total.at[m, core, :, l]
            start_copy(spot, spot, sent, landed, other)

    def stages(self, step):
        for unit in range(self.GRAIN[step]):
            self.stage(step, unit)

    def drain(self):
        for step in range(7):
            for unit in range(self.GRAIN[step]):
                wait_bytes(self.volume(step, unit), self.sent.at[step, unit])

    def greet(self, barrier):
        x, y, z, core = self.x, self.y, self.z, self.core
        peers = [device(x, y, z, 1 - core)]
        peers += [device(px, y, z, core) for px in self.x_peers()]
        peers += [device(x, py, z, core) for py in self.y_peers()]
        peers += [device(x, y, pz, core) for pz in self.z_peers()]
        for peer in peers:
            pl.semaphore_signal(barrier, inc=1, device_id=peer, device_id_type=MESH_ID)
        return len(peers)


PROBE_SUM_SCRATCH = [
    pltpu.VMEM((2, 256, 256), jnp.float32),
    pltpu.VMEM((2, 256, 256), jnp.float32),
    pltpu.VMEM((3, 2, 64, 256), jnp.float32),
    pltpu.VMEM((2, 64, 256), jnp.float32),
    pltpu.VMEM((7, 2, 8, 256), jnp.float32),
    pltpu.VMEM((12, 2, 8, 256), jnp.float32),
    pltpu.SemaphoreType.DMA((7, 4)),
    pltpu.SemaphoreType.DMA((7, 4)),
]


def whole_kernel(
    position, tile_in, probe_in, amplitude_in, table_in,
    grads, down_in, total,
    tile, probe, amplitude, table, loads,
    patch, moved_probe, wave, corner, left_corner, below, merged, side, own_spectrum, side_spectrum, spectrum, sent, landed,
    parts, side_out, side_in, down_out, back_sent, back_landed, *scratch,
):
    def load(source, target, index):
        copy = pltpu.make_async_copy(source, target, loads.at[index])
        copy.start()
        return copy

    row, z = lax.axis_index("row"), lax.axis_index("col")
    core = lax.rem(row, 2)
    up, down = (lax.rem(row + ROWS - 1, ROWS), z), (lax.rem(row + 1, ROWS), z)
    right = (row, lax.rem(z + 1, COLS))
    onward = (row, lax.rem(z + COLS - 1 + 2 * core, COLS))
    back = (row, lax.rem(z + 1 + (COLS - 2) * core, COLS))
    probe_total = ProbeSum(parts, total, *scratch)

    loading = [
        load(source, target, index)
        for index, (source, target) in enumerate(
            [(amplitude_in, amplitude), (tile_in, tile), (probe_in, probe), (table_in, table)]
        )
    ]
    barrier = pltpu.get_barrier_semaphore()
    count = probe_total.greet(barrier)
    for peer in (up, down):
        pl.semaphore_signal(barrier, inc=1, device_id=peer, device_id_type=MESH_ID)

    rows, lanes = iota(0), iota(1)
    first_row = lax.broadcasted_iota(jnp.int32, (8, WIDTH), 0) == 0
    corner[...] = jnp.where(first_row, position[0, 0] - row * WIDTH, position[0, 1] - z * WIDTH)
    to_combs = one_hot(lanes == 2 * lax.rem(rows, HALF) + rows // HALF)
    from_combs = one_hot(rows == 2 * lax.rem(lanes, HALF) + lanes // HALF)
    loading[0].wait()
    own_spectrum[...] = permute(to_combs, [amplitude[...]], from_combs)[0]
    for copy in loading[1:]:
        copy.wait()
    pl.semaphore_wait(barrier, count + 2)

    def chunk(index):
        layer, part, half = index // 4, (index // 2) % 2, index % 2
        return layer, part, pl.ds(half * HALF, HALF)

    copies = [start_copy(corner, left_corner, sent.at[16], landed.at[16], right)]
    for index in range(8):
        spot = chunk(index)
        copies.append(start_copy(tile.at[spot], below.at[spot], sent.at[index], landed.at[index], up))

    @pl.when(core == 1)
    def _():
        start_copy(own_spectrum, side_spectrum, sent.at[17], landed.at[17], right)

    wait_bytes(left_corner, landed.at[16])
    own, other = corner[...], left_corner[...]
    working = own + core * (other - own)
    handing = other + core * (own - other)
    row_start, col_start, hand_start = working[0:1, :], working[1:2, :], handing[0:1, :]
    own_columns = jnp.where(lanes >= col_start, 1, 0) != core

    for index in range(8):
        layer, part, span = chunk(index)
        wait_bytes(below.at[layer, part, span], landed.at[index])
        mine, under = tile[layer, part, span, :], below[layer, part, span, :]
        merged[layer, part, span, :] = jnp.where(rows[span.start : span.start + HALF] >= hand_start, mine, under)
        spot = merged.at[layer, part, span]
        copies.append(start_copy(spot, side.at[layer, part, span], sent.at[8 + index], landed.at[8 + index], onward))
        patch[layer, part, span, :] = jnp.where(rows[span.start : span.start + HALF] >= row_start, mine, under)
        if index == 3:
            shift_rows = one_hot(jnp.bitwise_and(rows - lanes - row_start, WIDTH - 1) == 0)
            shift_cols = one_hot(jnp.bitwise_and(lanes - rows - col_start, WIDTH - 1) == 0)
            planes = [probe[mode, part] for mode in range(2) for part in range(2)]
            for k, plane in enumerate(permute(shift_rows, planes, shift_cols)):
                moved_probe[k // 2, k % 2] = plane

    def patch_of(layer):
        for index in range(4):
            wait_bytes(side.at[chunk(4 * layer + index)], landed.at[8 + 4 * layer + index])
        pair = tuple(jnp.where(own_columns, patch[layer, part], side[layer, part]) for part in range(2))
        patch[layer, 0], patch[layer, 1] = pair
        return pair

    first = patch_of(0)
    waves = [times((moved_probe[mode, 0], moved_probe[mode, 1]), first) for mode in range(2)]
    for mode, pair in enumerate(unfold(both_sides(fold(waves), table, KERNEL))):
        wave[mode, 0], wave[mode, 1] = pair
    second = patch_of(1)

    @pl.when(core == 0)
    def _():
        spectrum[...] = own_spectrum[...]

    @pl.when(core == 1)
    def _():
        wait_bytes(side_spectrum, landed.at[17])
        spectrum[...] = side_spectrum[...]

    waves = [(wave[mode, 0], wave[mode, 1]) for mode in range(2)]
    far = in_combs(both_sides(fold([times(pair, second) for pair in waves]), table, DFT))
    intensity = far[0][0] * far[0][0] + far[0][1] * far[0][1] + (far[1][0] * far[1][0] + far[1][1] * far[1][1])
    weight = 2.0 - 2.0 * spectrum[...] * lax.rsqrt(intensity + intensity_floor)
    far = [(weight * re, weight * im) for re, im in far]
    slope = unfold(both_sides(comb_fields(far), table, DFT_BACK))

    def send_side(layer, terms):
        for part in range(2):
            grads[layer, part] = terms[0][part] + terms[1][part]
            side_out[layer, part] = jnp.where(own_columns, 0.0, grads[layer, part])
        copies.append(
            start_copy(side_out.at[layer], side_in.at[layer], back_sent.at[layer], back_landed.at[layer], back)
        )

    def send_down(layer):
        wait_bytes(side_in.at[layer], back_landed.at[layer])
        for part in range(2):
            mine = jnp.where(own_columns, grads[layer, part], 0.0)
            other = side_in[layer, part]
            down_out[layer, part] = jnp.where(rows < row_start, mine, 0.0) + jnp.where(rows < hand_start, other, 0.0)
            grads[layer, part] = jnp.where(rows < row_start, 0.0, mine) + jnp.where(rows < hand_start, 0.0, other)
        copies.append(
            start_copy(
                down_out.at[layer], down_in.at[layer], back_sent.at[2 + layer], back_landed.at[2 + layer], down
            )
        )

    def finish(layer):
        wait_bytes(down_in.at[layer], back_landed.at[2 + layer])

    send_side(1, [times_conj(slope[mode], waves[mode]) for mode in range(2)])
    shift_rows = one_hot(jnp.bitwise_and(lanes - rows - row_start, WIDTH - 1) == 0)
    shift_cols = one_hot(jnp.bitwise_and(rows - lanes - col_start, WIDTH - 1) == 0)
    first, second = (patch[0, 0], patch[0, 1]), (patch[1, 0], patch[1, 1])
    terms = []
    for mode in range(2):
        bent = unfold(both_sides(fold([times_conj(slope[mode], second)]), table, KERNEL_BACK))[0]
        if mode == 1:
            probe_total.stage(1, 0)
            probe_total.stage(1, 1)
        for part, plane in enumerate(permute(shift_rows, list(times_conj(bent, first)), shift_cols)):
            parts[mode, part] = plane
        probe_total.stage(0, 2 * mode)
        probe_total.stage(0, 2 * mode + 1)
        terms.append(times_conj(bent, (moved_probe[mode, 0], moved_probe[mode, 1])))
    send_side(0, terms)
    probe_total.stage(1, 2)
    probe_total.stage(1, 3)
    send_down(1)
    probe_total.stages(2)
    probe_total.stages(3)
    send_down(0)
    finish(1)
    probe_total.stages(4)
    probe_total.stages(5)
    finish(0)
    probe_total.stages(6)
    probe_total.stages(7)
    probe_total.drain()
    for copy in copies:
        copy.wait_send()

    @pl.when(core == 1)
    def _():
        wait_bytes(side_spectrum, sent.at[17])


def on_device(object_field, probe, scan_positions, amplitudes):
    full, plane = (2, 2, WIDTH, WIDTH), (WIDTH, WIDTH)
    vmem = lambda *dims: pltpu.VMEM(dims, f32)
    anywhere = pl.BlockSpec(memory_space=pltpu.HBM)
    table = jnp.asarray(tables())
    grads, arrived, total = pl.pallas_call(
        whole_kernel,
        out_shape=[jax.ShapeDtypeStruct(full, f32)] * 3,
        in_specs=[pl.BlockSpec(memory_space=pltpu.SMEM)] + [anywhere] * 4,
        out_specs=[pl.BlockSpec(memory_space=pltpu.VMEM)] * 3,
        scratch_shapes=[
            vmem(*full), vmem(*full), vmem(*plane), pltpu.VMEM(table.shape, bf16), pltpu.SemaphoreType.DMA((4,)),
            vmem(*full), vmem(*full), vmem(*full),
            pltpu.VMEM((8, WIDTH), jnp.int32), pltpu.VMEM((8, WIDTH), jnp.int32),
            vmem(*full), vmem(*full), vmem(*full), vmem(*plane), vmem(*plane), vmem(*plane),
            pltpu.SemaphoreType.DMA((18,)), pltpu.SemaphoreType.DMA((18,)),
            vmem(*full), vmem(*full), vmem(*full), vmem(*full),
            pltpu.SemaphoreType.DMA((4,)), pltpu.SemaphoreType.DMA((4,)),
            *PROBE_SUM_SCRATCH,
        ],
        compiler_params=pltpu.CompilerParams(collective_id=0, has_side_effects=True, vmem_limit_bytes=50 << 20),
    )(scan_positions.reshape(1, 2), object_field, probe, amplitudes[0, 0, 0], table)
    return grads + arrived, total * (1.0 / math.sqrt(ROWS * COLS))


def solution(mesh):
    in_specs = (
        P(None, None, "row", "col"),
        P(),
        P("row", "col", None, None),
        P("row", "col", None, None, None),
    )
    out_specs = (P(None, None, "row", "col"), P())
    return jax.shard_map(
        on_device, mesh=mesh, in_specs=in_specs, out_specs=out_specs, check_vma=False
    )
```

time: 93.4 us -> 82.3 us (0.88)
  local copies, waits for them, and re-layouts: 10.6 us -> 1.6 us
  Pallas kernels: 81.7 us -> 77.7 us
  other arithmetic: 0.08 us -> 2.18 us
    unnamed x30 -> x4, local copies, waits for them, and re-layouts: 10.5 us -> 1.6 us
    pallas_call x2 -> x1, Pallas kernels: 81.7 us -> 77.7 us  [on_device(): pl.pallas_call(whole_kernel, out_shape=[jax.ShapeDtypeStruct(full, f32)]...]
    add x0 -> x1, other arithmetic: none -> 1.11 us  [on_device(): return (grads + arrived, total * (1.0 / math.sqrt(ROWS * COLS)))]
    mul x0 -> x1, other arithmetic: none -> 1.07 us  [on_device(): return (grads + arrived, total * (1.0 / math.sqrt(ROWS * COLS)))]
where the time goes in v3:
time: 82.3 us; the launch traced here: 82.1 us
  Pallas kernels  77.7 us (94%)
  other arithmetic  2.18 us (3%)
  local copies, waits for them, and re-layouts  1.6 us (2%)
    pallas_call x1, Pallas kernels, on_device(): pl.pallas_call(whole_kernel, out_shape=[jax.ShapeDtypeStruct(full, f32)]...  77.7 us

profile of v3, /device:TPU:1, one launch (start us, length us, event | category | flops | bytes accessed | tf_op | source)
XLA Modules:
  0.0 82.1 jit_solution(10124313681256427862)
XLA Ops:
  0.6 0.0 copy-start
  0.6 0.9 %copy-done = f32[1,1,1,256,256]{4,3,2,1,0:T(8,128)S(1)} copy-done((f32[1,1,1,256,256]{4,3,2,1,0:T(8,128)S(1)}, f32[1,1,1,256,256]{4,3,2,1,0:T(8,128)}, u32[]{:S(2)}) %copy-start) | copy-done | bytes 262168
  1.6 0.0 copy-start.1
  1.6 0.7 copy-done.1
  2.2 77.7 %shard_map.68 = (f32[2,2,256,256]{3,2,1,0:T(8,128)S(1)}, f32[2,2,256,256]{3,2,1,0:T(8,128)S(1)}, f32[2,2,256,256]{3,2,1,0:T(8,128)S(1)}) custom-call(s32[1,2]{1,0:T(1,128)S(1)} %bitcast.3, f32[2,2,256,256]{3,2,1,0:T(8,128)} %tile_in.1, f32[2,2,256,256]{3,2,1,0:T(8,128)} %probe_in.1, f32[256,256]{1,0:T(8,128)S(1)} %bitcast.2, ...), custom_call_target="tpu_custom_call" | custom-call | tf_op jit(solution)/shard_map/pallas_call | solution.py:482
  79.9 1.1 %add.3 = f32[2,2,256,256]{3,2,1,0:T(8,128)} add(f32[2,2,256,256]{3,2,1,0:T(8,128)S(1)} %get-tuple-element.5, f32[2,2,256,256]{3,2,1,0:T(8,128)S(1)} %get-tuple-element.6) | non-fusion elementwise | flops 262144 | bytes 3145728 | tf_op jit(solution)/shard_map/add | solution.py:499
  81.0 1.1 %broadcast_multiply_fusion = f32[2,2,256,256]{3,2,1,0:T(8,128)} fusion(f32[2,2,256,256]{3,2,1,0:T(8,128)S(1)} %get-tuple-element.7), kind=kLoop, calls=%fused_computation | loop fusion | flops 262144 | bytes 2097152 | tf_op jit(solution)/shard_map/mul | solution.py:499
Async XLA Ops:
  0.6 1.0 %copy-start = (f32[1,1,1,256,256]{4,3,2,1,0:T(8,128)S(1)}, f32[1,1,1,256,256]{4,3,2,1,0:T(8,128)}, u32[]{:S(2)}) copy-start(f32[1,1,1,256,256]{4,3,2,1,0:T(8,128)} %param.8) | copy-start | bytes 786436
  1.6 0.7 copy-start.1

commit v4 on v3

--- a/solution.py
+++ b/solution.py
@@ -263,7 +263,7 @@
             piece = self.from_z[0, m, :, l]
             for d in range(1, 12):
                 piece = piece + self.from_z[d, m, :, l]
-            self.total[m, core, mine, l] = piece
+            self.total[m, core, mine, l] = piece * (1.0 / math.sqrt(ROWS * COLS))
             spot = self.total.at[m, core, mine, l]
             for py in self.y_peers():
                 start_copy(spot, spot, sent, landed, device(x, py, z, core))
@@ -455,8 +455,8 @@
     send_side(0, terms)
     probe_total.stage(1, 2)
     probe_total.stage(1, 3)
+    probe_total.stages(2)
     send_down(1)
-    probe_total.stages(2)
     probe_total.stages(3)
     send_down(0)
     finish(1)
@@ -474,11 +474,29 @@
         wait_bytes(side_spectrum, sent.at[17])
 
 
+def last_kernel(grads, arrived, total, object_gradient, probe_gradient, summed, written):
+    copies = []
+
+    def write(source, target):
+        copies.append(pltpu.make_async_copy(source, target, written.at[len(copies)]))
+        copies[-1].start()
+
+    spots = [(first, second) for first in range(2) for second in range(2)]
+    for spot in spots:
+        write(total.at[spot], probe_gradient.at[spot])
+    for spot in spots:
+        summed[spot] = grads[spot] + arrived[spot]
+        write(summed.at[spot], object_gradient.at[spot])
+    for copy in copies:
+        copy.wait()
+
+
 def on_device(object_field, probe, scan_positions, amplitudes):
     full, plane = (2, 2, WIDTH, WIDTH), (WIDTH, WIDTH)
     vmem = lambda *dims: pltpu.VMEM(dims, f32)
     anywhere = pl.BlockSpec(memory_space=pltpu.HBM)
     table = jnp.asarray(tables())
+    operands = (scan_positions.reshape(1, 2), object_field, probe, amplitudes[0, 0, 0], table)
     grads, arrived, total = pl.pallas_call(
         whole_kernel,
         out_shape=[jax.ShapeDtypeStruct(full, f32)] * 3,
@@ -494,9 +512,18 @@
             pltpu.SemaphoreType.DMA((4,)), pltpu.SemaphoreType.DMA((4,)),
             *PROBE_SUM_SCRATCH,
         ],
-        compiler_params=pltpu.CompilerParams(collective_id=0, has_side_effects=True, vmem_limit_bytes=50 << 20),
-    )(scan_positions.reshape(1, 2), object_field, probe, amplitudes[0, 0, 0], table)
-    return grads + arrived, total * (1.0 / math.sqrt(ROWS * COLS))
+        compiler_params=pltpu.CompilerParams(collective_id=0, has_side_effects=True, vmem_limit_bytes=40 << 20),
+    )(*(pltpu.with_memory_space_constraint(x, pltpu.HBM) for x in operands))
+    return tuple(
+        pl.pallas_call(
+            last_kernel,
+            out_shape=[jax.ShapeDtypeStruct(full, f32)] * 2,
+            in_specs=[pl.BlockSpec(memory_space=pltpu.VMEM)] * 3,
+            out_specs=[anywhere] * 2,
+            scratch_shapes=[vmem(*full), pltpu.SemaphoreType.DMA((8,))],
+            compiler_params=pltpu.CompilerParams(vmem_limit_bytes=8 << 20),
+        )(grads, arrived, total)
+    )
 
 
 def solution(mesh):

time: 82.3 us -> 80.4 us (0.977)
  other arithmetic: 2.18 us -> 0 us
  Pallas kernels: 77.7 us -> 79.6 us
  local copies, waits for them, and re-layouts: 1.6 us -> 0 us
    unnamed x4 -> x0, local copies, waits for them, and re-layouts: 1.6 us -> none
    pallas_call x0 -> x1, Pallas kernels: none -> 1.38 us  [on_device(): pl.pallas_call(last_kernel, out_shape=[jax.ShapeDtypeStruct(full, f32)] *...]
    add x1 -> x0, other arithmetic: 1.11 us -> none  [on_device(): return (grads + arrived, total * (1.0 / math.sqrt(ROWS * COLS)))]
    mul x1 -> x0, other arithmetic: 1.07 us -> none  [on_device(): return (grads + arrived, total * (1.0 / math.sqrt(ROWS * COLS)))]
where the time goes in v4:
time: 80.4 us; the launch traced here: 80.2 us
  Pallas kernels  79.6 us (99%)
    pallas_call x1, Pallas kernels, on_device(): pl.pallas_call(whole_kernel, out_shape=[jax.ShapeDtypeStruct(full, f32)]...  78.2 us

profile of v4, /device:TPU:1, one launch (start us, length us, event | category | flops | bytes accessed | tf_op | source)
XLA Modules:
  0.0 80.2 jit_solution(1466520394832970102)
XLA Ops:
  0.6 78.2 %shard_map.68 = (f32[2,2,256,256]{3,2,1,0:T(8,128)S(1)}, f32[2,2,256,256]{3,2,1,0:T(8,128)S(1)}, f32[2,2,256,256]{3,2,1,0:T(8,128)S(1)}) custom-call(s32[1,2]{1,0:T(1,128)} %bitcast.3, f32[2,2,256,256]{3,2,1,0:T(8,128)} %tile_in.1, f32[2,2,256,256]{3,2,1,0:T(8,128)} %probe_in.1, f32[256,256]{1,0:T(8,128)} %bitcast.2, ...), custom_call_target="tpu_custom_call" | custom-call | tf_op jit(solution)/shard_map/pallas_call | solution.py:500
  78.9 1.4 %shard_map.69 = (f32[2,2,256,256]{3,2,1,0:T(8,128)}, f32[2,2,256,256]{3,2,1,0:T(8,128)}) custom-call(f32[2,2,256,256]{3,2,1,0:T(8,128)S(1)} %get-tuple-element.5.grads, f32[2,2,256,256]{3,2,1,0:T(8,128)S(1)} %get-tuple-element.6.arrived, f32[2,2,256,256]{3,2,1,0:T(8,128)S(1)} %get-tuple-element.7.total), custom_call_target="tpu_custom_call" | custom-call | tf_op jit(solution)/shard_map/pallas_call | solution.py:518

commit v5 on v4

--- a/solution.py
+++ b/solution.py
@@ -284,15 +284,31 @@
             for unit in range(self.GRAIN[step]):
                 wait_bytes(self.volume(step, unit), self.sent.at[step, unit])
 
+    REACH = (2, 4, 6)
+
+    def beside(self, axis, by):
+        x, y, z, core = self.x, self.y, self.z, self.core
+        if axis == 0:
+            return device(lax.rem(x + 4 + by, 4), y, z, core)
+        if axis == 1:
+            return device(x, lax.rem(y + 8 + by, 8), z, core)
+        return device(x, y, lax.rem(z + 12 + by, 12), core)
+
     def greet(self, barrier):
-        x, y, z, core = self.x, self.y, self.z, self.core
-        peers = [device(x, y, z, 1 - core)]
-        peers += [device(px, y, z, core) for px in self.x_peers()]
-        peers += [device(x, py, z, core) for py in self.y_peers()]
-        peers += [device(x, y, pz, core) for pz in self.z_peers()]
+        peers = [device(self.x, self.y, self.z, 1 - self.core)]
+        peers += [self.beside(axis, by) for axis in range(3) for by in (1, -1)]
         for peer in peers:
             pl.semaphore_signal(barrier, inc=1, device_id=peer, device_id_type=MESH_ID)
         return len(peers)
+
+    def pass_word(self, words, distance):
+        for axis, reach in enumerate(self.REACH):
+            for way, by in enumerate((1, -1)):
+                if 2 < distance <= reach + 1:
+                    pl.semaphore_wait(words.at[axis, way, distance - 3], 1)
+                if distance <= reach:
+                    word = words.at[axis, way, distance - 2]
+                    pl.semaphore_signal(word, inc=1, device_id=self.beside(axis, by), device_id_type=MESH_ID)
 
 
 PROBE_SUM_SCRATCH = [
@@ -311,7 +327,7 @@
     position, tile_in, probe_in, amplitude_in, table_in,
     grads, down_in, total,
     tile, probe, amplitude, table, loads,
-    patch, moved_probe, wave, corner, left_corner, below, merged, side, own_spectrum, side_spectrum, spectrum, sent, landed,
+    patch, moved_probe, wave, corner, left_corner, below, merged, side, own_spectrum, side_spectrum, spectrum, sent, landed, words,
     parts, side_out, side_in, down_out, back_sent, back_landed, *scratch,
 ):
     def load(source, target, index):
@@ -362,6 +378,7 @@
     def _():
         start_copy(own_spectrum, side_spectrum, sent.at[17], landed.at[17], right)
 
+    probe_total.pass_word(words, 2)
     wait_bytes(left_corner, landed.at[16])
     own, other = corner[...], left_corner[...]
     working = own + core * (other - own)
@@ -377,6 +394,8 @@
         spot = merged.at[layer, part, span]
         copies.append(start_copy(spot, side.at[layer, part, span], sent.at[8 + index], landed.at[8 + index], onward))
         patch[layer, part, span, :] = jnp.where(rows[span.start : span.start + HALF] >= row_start, mine, under)
+        if index % 2:
+            probe_total.pass_word(words, 3 + index // 2)
         if index == 3:
             shift_rows = one_hot(jnp.bitwise_and(rows - lanes - row_start, WIDTH - 1) == 0)
             shift_cols = one_hot(jnp.bitwise_and(lanes - rows - col_start, WIDTH - 1) == 0)
@@ -395,6 +414,7 @@
     waves = [times((moved_probe[mode, 0], moved_probe[mode, 1]), first) for mode in range(2)]
     for mode, pair in enumerate(unfold(both_sides(fold(waves), table, KERNEL))):
         wave[mode, 0], wave[mode, 1] = pair
+    probe_total.pass_word(words, 7)
     second = patch_of(1)
 
     @pl.when(core == 0)
@@ -507,7 +527,7 @@
             vmem(*full), vmem(*full), vmem(*full),
             pltpu.VMEM((8, WIDTH), jnp.int32), pltpu.VMEM((8, WIDTH), jnp.int32),
             vmem(*full), vmem(*full), vmem(*full), vmem(*plane), vmem(*plane), vmem(*plane),
-            pltpu.SemaphoreType.DMA((18,)), pltpu.SemaphoreType.DMA((18,)),
+            pltpu.SemaphoreType.DMA((18,)), pltpu.SemaphoreType.DMA((18,)), pltpu.SemaphoreType.REGULAR((3, 2, 5)),
             vmem(*full), vmem(*full), vmem(*full), vmem(*full),
             pltpu.SemaphoreType.DMA((4,)), pltpu.SemaphoreType.DMA((4,)),
             *PROBE_SUM_SCRATCH,

time: 80.4 us -> 79.5 us (0.989)
    pallas_call x1, Pallas kernels: 78.2 us -> 77.4 us  [on_device(): pl.pallas_call(whole_kernel, out_shape=[jax.ShapeDtypeStruct(full, f32)]...]
where the time goes in v5:
time: 79.5 us; the launch traced here: 79.4 us
  Pallas kernels  78.8 us (99%)
    pallas_call x1, Pallas kernels, on_device(): pl.pallas_call(whole_kernel, out_shape=[jax.ShapeDtypeStruct(full, f32)]...  77.4 us

profile of v5, /device:TPU:1, one launch (start us, length us, event | category | flops | bytes accessed | tf_op | source)
XLA Modules:
  0.0 79.4 jit_solution(1273658191571335324)
XLA Ops:
  0.6 77.4 %shard_map.68 = (f32[2,2,256,256]{3,2,1,0:T(8,128)S(1)}, f32[2,2,256,256]{3,2,1,0:T(8,128)S(1)}, f32[2,2,256,256]{3,2,1,0:T(8,128)S(1)}) custom-call(s32[1,2]{1,0:T(1,128)} %bitcast.3, f32[2,2,256,256]{3,2,1,0:T(8,128)} %tile_in.1, f32[2,2,256,256]{3,2,1,0:T(8,128)} %probe_in.1, f32[256,256]{1,0:T(8,128)} %bitcast.2, ...), custom_call_target="tpu_custom_call" | custom-call | tf_op jit(solution)/shard_map/pallas_call | solution.py:520
  78.0 1.4 %shard_map.69 = (f32[2,2,256,256]{3,2,1,0:T(8,128)}, f32[2,2,256,256]{3,2,1,0:T(8,128)}) custom-call(f32[2,2,256,256]{3,2,1,0:T(8,128)S(1)} %get-tuple-element.5.grads, f32[2,2,256,256]{3,2,1,0:T(8,128)S(1)} %get-tuple-element.6.arrived, f32[2,2,256,256]{3,2,1,0:T(8,128)S(1)} %get-tuple-element.7.total), custom_call_target="tpu_custom_call" | custom-call | tf_op jit(solution)/shard_map/pallas_call | solution.py:538

commit v6 on v5

--- a/solution.py
+++ b/solution.py
@@ -187,13 +187,13 @@
         self.arrived = set()
 
     def x_peers(self):
-        return [lax.rem(self.x + d, 4) for d in range(1, 4)]
+        return [lax.rem(self.x + d, 4) for d in (2, 1, 3)]
 
     def y_peers(self):
-        return [lax.rem(self.y + d, 8) for d in range(1, 8)]
+        return [lax.rem(self.y + d, 8) for d in (4, 3, 5, 2, 6, 1, 7)]
 
     def z_peers(self):
-        return [lax.rem(self.z + d, 12) for d in range(1, 12)]
+        return [lax.rem(self.z + d, 12) for d in (6, 5, 7, 4, 8, 3, 9, 2, 10, 1, 11)]
 
     def cut(self, step, unit):
         grain = self.GRAIN[step]
@@ -396,7 +396,7 @@
         patch[layer, part, span, :] = jnp.where(rows[span.start : span.start + HALF] >= row_start, mine, under)
         if index % 2:
             probe_total.pass_word(words, 3 + index // 2)
-        if index == 3:
+        if index == 7:
             shift_rows = one_hot(jnp.bitwise_and(rows - lanes - row_start, WIDTH - 1) == 0)
             shift_cols = one_hot(jnp.bitwise_and(lanes - rows - col_start, WIDTH - 1) == 0)
             planes = [probe[mode, part] for mode in range(2) for part in range(2)]
@@ -476,15 +476,15 @@
     probe_total.stage(1, 2)
     probe_total.stage(1, 3)
     probe_total.stages(2)
+    probe_total.stages(3)
     send_down(1)
-    probe_total.stages(3)
-    send_down(0)
-    finish(1)
     probe_total.stages(4)
     probe_total.stages(5)
+    send_down(0)
+    probe_total.stages(6)
+    finish(1)
+    probe_total.stages(7)
     finish(0)
-    probe_total.stages(6)
-    probe_total.stages(7)
     probe_total.drain()
     for copy in copies:
         copy.wait_send()

time: 79.5 us -> 81.6 us (1.026)
  Pallas kernels: 78.8 us -> 80.4 us
    pallas_call x1, Pallas kernels: 77.4 us -> 79 us  [on_device(): pl.pallas_call(whole_kernel, out_shape=[jax.ShapeDtypeStruct(full, f32)]...]
where the time goes in v6:
time: 81.6 us; the launch traced here: 81 us
  Pallas kernels  80.4 us (99%)
    pallas_call x1, Pallas kernels, on_device(): pl.pallas_call(whole_kernel, out_shape=[jax.ShapeDtypeStruct(full, f32)]...  79 us

profile of v6, /device:TPU:1, one launch (start us, length us, event | category | flops | bytes accessed | tf_op | source)
XLA Modules:
  0.0 81.0 jit_solution(2015042045070282868)
XLA Ops:
  0.6 79.0 %shard_map.68 = (f32[2,2,256,256]{3,2,1,0:T(8,128)S(1)}, f32[2,2,256,256]{3,2,1,0:T(8,128)S(1)}, f32[2,2,256,256]{3,2,1,0:T(8,128)S(1)}) custom-call(s32[1,2]{1,0:T(1,128)} %bitcast.3, f32[2,2,256,256]{3,2,1,0:T(8,128)} %tile_in.1, f32[2,2,256,256]{3,2,1,0:T(8,128)} %probe_in.1, f32[256,256]{1,0:T(8,128)} %bitcast.2, ...), custom_call_target="tpu_custom_call" | custom-call | tf_op jit(solution)/shard_map/pallas_call | solution.py:520
  79.6 1.4 %shard_map.69 = (f32[2,2,256,256]{3,2,1,0:T(8,128)}, f32[2,2,256,256]{3,2,1,0:T(8,128)}) custom-call(f32[2,2,256,256]{3,2,1,0:T(8,128)S(1)} %get-tuple-element.5.grads, f32[2,2,256,256]{3,2,1,0:T(8,128)S(1)} %get-tuple-element.6.arrived, f32[2,2,256,256]{3,2,1,0:T(8,128)S(1)} %get-tuple-element.7.total), custom_call_target="tpu_custom_call" | custom-call | tf_op jit(solution)/shard_map/pallas_call | solution.py:538
